TPU v7x, 512 devices: a whole 4x4x16 slice. The times are simulated.
512 devices in a mesh: mp: 64 (over y, z), narrow: 8 (over x, core).
Axes of the slice: x: 4, y: 4, z: 16, core: 2. Of those that a mesh axis runs over, the one named last changes fastest.
Arguments:
- inputs: bfloat16 [512, 8192], P('mp', 'narrow'), may hold values from -36 to 36, as said below
- out_grad: bfloat16 [512, 8192], P('mp', 'narrow'), may hold values from -36 to 36, as said below
- w_in: bfloat16 [8192, 32768], P('narrow', 'mp'), may hold values from -0.0625 to 0.0625
- w_out: bfloat16 [32768, 8192], P('mp', 'narrow'), may hold values from -0.03125 to 0.03125
- row_in: float32 [8192], P('narrow'), may hold values from 0.1 to 40, as said below
- col_in: float32 [32768], P('mp'), may hold values from 0.1 to 40, as said below
- row_out: float32 [32768], P('mp'), may hold values from 0.1 to 40, as said below
- col_out: float32 [8192], P('narrow'), may hold values from 0.1 to 40, as said below
Outputs:
- input_grad: bfloat16 [512, 8192], P('mp', 'narrow')
- update_in: bfloat16 [8192, 32768], P('narrow', 'mp')
- update_out: bfloat16 [32768, 8192], P('mp', 'narrow')
- row_in_new: float32 [8192], P('narrow')
- col_in_new: float32 [32768], P('mp')
- row_out_new: float32 [32768], P('mp')
- col_out_new: float32 [8192], P('narrow')
Inputs may be any that keep to these rules, and one draw needn't show every extreme that they name: `inputs`: real values. `out_grad`: real values. `row_in`: positive moments. `col_in`: positive moments. `row_out`: positive moments. `col_out`: positive moments.
All inputs are finite; a program needn't handle non-finite values.
Results may differ from a plain program's by a relative error of at most 0.005.
Values may be sent and summed in bfloat16 or wider, within the bound.
A program may use at most 64 MiB of HBM per device.

v0:
```python
import jax
import jax.numpy as jnp
from jax import lax
from jax.sharding import PartitionSpec as P

D = 8192
FF = 32768


decay_rate = 0.8
epsilon = 1e-06
clip_floor = 0.01


def silu_grad(preact):
    sigma = jax.nn.sigmoid(preact)
    return sigma * (1.0 + preact * (1.0 - sigma))


def activate(preact, upstream):
    activation = jax.nn.silu(preact).astype(jnp.bfloat16)
    hidden_grad = (upstream * silu_grad(preact)).astype(jnp.bfloat16)
    return (activation, hidden_grad)


def per_device(inputs, out_grad, w_in, w_out, row_in, col_in, row_out, col_out):
    x_all, dy_all = (
        lax.all_gather(inputs, "mp", axis=0, tiled=True),
        lax.all_gather(out_grad, "mp", axis=0, tiled=True),
    )
    pre_local = jnp.dot(x_all, w_in, preferred_element_type=jnp.float32)
    up_local = lax.dot_general(
        dy_all, w_out, (((1,), (1,)), ((), ())), preferred_element_type=jnp.float32
    )
    preact, upstream = lax.psum((pre_local, up_local), "narrow")
    activation, hidden_grad = activate(preact, upstream)
    grad_out = lax.dot_general(
        activation, dy_all, (((0,), (0,)), ((), ())), preferred_element_type=jnp.float32
    )
    grad_in = lax.dot_general(
        x_all, hidden_grad, (((0,), (0,)), ((), ())), preferred_element_type=jnp.float32
    )
    input_grad = lax.psum_scatter(
        lax.dot_general(
            hidden_grad, w_in, (((1,), (1,)), ((), ())), preferred_element_type=jnp.float32
        ),
        "mp",
        scatter_dimension=0,
        tiled=True,
    ).astype(jnp.bfloat16)
    square_in = grad_in * grad_in + epsilon
    square_out = grad_out * grad_out + epsilon
    in_rowsum, out_colsum = lax.psum(
        (jnp.sum(square_in, axis=1), jnp.sum(square_out, axis=0)), "mp"
    )
    in_colsum, out_rowsum = lax.psum(
        (jnp.sum(square_in, axis=0), jnp.sum(square_out, axis=1)), "narrow"
    )
    row_in_new = decay_rate * row_in + (1.0 - decay_rate) * (in_rowsum / FF)
    col_in_new = decay_rate * col_in + (1.0 - decay_rate) * (in_colsum / D)
    row_out_new = decay_rate * row_out + (1.0 - decay_rate) * (out_rowsum / D)
    col_out_new = decay_rate * col_out + (1.0 - decay_rate) * (out_colsum / FF)
    step_in = grad_in * lax.rsqrt(row_in_new[:, None] * col_in_new[None, :])
    step_out = grad_out * lax.rsqrt(row_out_new[:, None] * col_out_new[None, :])
    norm_in, norm_out = lax.psum(
        (jnp.sum(step_in * step_in), jnp.sum(step_out * step_out)), ("mp", "narrow")
    )
    entry_count = float(D) * float(FF)
    rms_in = jnp.sqrt(norm_in / entry_count)
    rms_out = jnp.sqrt(norm_out / entry_count)
    update_in = (step_in / jnp.maximum(clip_floor, rms_in)).astype(jnp.bfloat16)
    update_out = (step_out / jnp.maximum(clip_floor, rms_out)).astype(jnp.bfloat16)
    return (input_grad, update_in, update_out, row_in_new, col_in_new, row_out_new, col_out_new)


def solution(mesh):
    placed = (
        P("mp", "narrow"),
        P("mp", "narrow"),
        P("narrow", "mp"),
        P("mp", "narrow"),
        P("narrow"),
        P("mp"),
        P("mp"),
        P("narrow"),
    )
    return jax.shard_map(
        per_device,
        mesh=mesh,
        in_specs=placed,
        out_specs=(
            P("mp", "narrow"),
            P("narrow", "mp"),
            P("mp", "narrow"),
            P("narrow"),
            P("mp"),
            P("mp"),
            P("narrow"),
        ),
        check_vma=False,
    )
```

profile of v0, /device:TPU:1, one launch (start us, length us, event | category | flops | bytes accessed | tf_op | source)
XLA Modules:
  0.0 1069.4 jit_solution(12875801889576855448)
XLA Ops:
  7.2 0.0 copy-start
  7.2 0.0 all-gather.3.cloned.1.call-start
  7.2 0.7 all-gather.3.cloned.1.call-update
  7.9 0.0 all-gather.5.cloned.1.call-start
  8.0 0.7 all-gather.5.cloned.1.call-update
  8.7 0.0 all-reduce.6.cloned.1.call-start
  8.7 137.1 %all-gather.3.cloned.1.call-done = bf16[512,1024]{1,0:T(8,128)(2,1)} async-done(((bf16[8,1024]{1,0:T(8,128)(2,1)}), bf16[512,1024]{1,0:T(8,128)(2,1)}) %all-gather.3.cloned.1.call-update) | async-done | bytes 1048592 | tf_op jit(solution)/shard_map/all_gather | solution.py:29
  145.8 3.3 fusion.8
  149.0 134.8 %all-gather.5.cloned.1.call-done = bf16[512,1024]{1,0:T(8,128)(2,1)} async-done(((bf16[8,1024]{1,0:T(8,128)(2,1)}), bf16[512,1024]{1,0:T(8,128)(2,1)}) %all-gather.5.cloned.1.call-update) | async-done | bytes 1048592 | tf_op jit(solution)/shard_map/all_gather | solution.py:28
  283.8 0.0 copy-done
  283.8 2.9 fusion.9
  286.7 0.0 all-reduce.6.cloned.1.call-update
  286.7 0.0 reduce-scatter.2.cloned.1.call-start
  286.8 85.1 %all-reduce.6.cloned.1.call-done = (f32[512,512]{1,0:T(8,128)}, f32[512,512]{1,0:T(8,128)}) async-done(((f32[512,512]{1,0:T(8,128)}, f32[512,512]{1,0:T(8,128)}), (f32[512,512]{1,0:T(8,128)}, f32[512,512]{1,0:T(8,128)})) %all-reduce.6.cloned.1.call-update) | async-done | bytes 2097168 | tf_op jit(solution)/shard_map/psum | solution.py:35
  371.9 1.9 multiply_convert_fusion.1
  373.8 0.0 copy-start.3
  373.8 0.8 copy-done.3
  374.6 2.1 fusion.10
  376.7 0.0 reduce-scatter.2.cloned.1.call-update
  376.7 0.0 copy-start.4
  376.7 0.0 copy-start.13
  376.7 2.4 fusion.4
  379.1 0.0 copy-done.4
  379.1 0.0 copy-done.13
  379.1 0.0 copy-start.11
  379.1 0.0 copy-start.12
  379.1 0.0 copy-start.9
  379.1 0.0 copy-start.10
  379.2 2.1 fusion.2
  381.3 118.7 %all-reduce.1 = (f32[1024]{0:T(1024)S(1)}, f32[1024]{0:T(1024)S(1)}) all-reduce(f32[1024]{0:T(1024)S(1)} %get-tuple-element.16, f32[1024]{0:T(1024)S(1)} %get-tuple-element.15), channel_id=1, replica_groups=mesh['mp'=64,'narrow'=8] {'mp'}, use_global_device_ids=true, to_apply=%region_4.5 | all-reduce | flops 2048 | bytes 16384 | tf_op jit(solution)/shard_map/psum | solution.py:53
  500.0 41.9 %all-reduce.2 = (f32[512]{0:T(512)S(1)}, f32[512]{0:T(512)S(1)}) all-reduce(f32[512]{0:T(512)S(1)} %get-tuple-element.17, f32[512]{0:T(512)S(1)} %get-tuple-element.14), channel_id=1, replica_groups=mesh['mp'=64,'narrow'=8] {'narrow'}, use_global_device_ids=true, to_apply=%region_6.7 | all-reduce | flops 1024 | bytes 8192 | tf_op jit(solution)/shard_map/psum | solution.py:56
  541.9 0.0 copy-start.1
  541.9 0.0 copy-done.11
  541.9 0.0 copy-done.12
  541.9 0.0 copy-start.8
  541.9 0.0 copy-start.7
  541.9 0.0 copy-done.9
  541.9 0.0 copy-done.10
  542.0 0.0 copy-start.6
  542.0 0.0 copy-start.5
  542.0 1.5 multiply_reduce_fusion.1
  543.5 0.0 copy-done.1
  543.5 1.5 multiply_reduce_fusion
  545.0 99.4 %all-reduce = (f32[]{:T(128)}, f32[]{:T(128)}) all-reduce(f32[]{:T(128)} %multiply_reduce_fusion.1, f32[]{:T(128)} %multiply_reduce_fusion), channel_id=1, replica_groups=mesh['mp'=64,'narrow'=8] {'mp','narrow'}, use_global_device_ids=true, to_apply=%region_8.9 | all-reduce | flops 2 | bytes 16 | tf_op jit(solution)/shard_map/psum | solution.py:65
  645.8 0.0 copy-done.8
  645.8 0.0 copy-done.6
  645.8 1.4 divide_convert_fusion.1
  647.1 0.0 copy-start.2
  647.1 2.4 copy.15
  649.6 0.0 copy-done.7
  649.6 0.0 copy-done.5
  649.6 0.0 copy-done.2
  649.6 1.4 divide_convert_fusion
  650.9 410.5 %reduce-scatter.2.cloned.1.call-done = f32[8,1024]{1,0:T(8,128)} async-done(((f32[512,1024]{1,0:T(8,128)}), f32[8,1024]{1,0:T(8,128)}) %reduce-scatter.2.cloned.1.call-update) | async-done | bytes 32784 | tf_op jit(solution)/shard_map/reduce_scatter | solution.py:43
  1061.5 1.4 convert_element_type.16
  (2 shorter events, 0.0 us)
Async XLA Ops:
  7.2 276.6 %copy-start = (bf16[1024,512]{1,0:T(8,128)(2,1)S(1)}, bf16[1024,512]{1,0:T(8,128)(2,1)}, u32[]{:S(2)}) copy-start(bf16[1024,512]{1,0:T(8,128)(2,1)} %param.10) | copy-start | bytes 3145732
  7.2 138.6 %all-gather.3.cloned.1.call-start = ((), (), s32[]{:S(2)}) async-start(), calls=%async_computation.1 | async-start | bytes 1064960 | tf_op jit(solution)/shard_map/all_gather | solution.py:29
  7.9 275.9 %all-gather.5.cloned.1.call-start = ((), (), s32[]{:S(2)}) async-start(), calls=%async_computation.2 | async-start | bytes 1064960 | tf_op jit(solution)/shard_map/all_gather | solution.py:28
  8.7 363.2 %all-reduce.6.cloned.1.call-start = ((), (), s32[]{:S(2)}) async-start(), calls=%async_computation.4 | async-start | bytes 4194304 | tf_op jit(solution)/shard_map/psum | solution.py:35
  286.7 774.7 %reduce-scatter.2.cloned.1.call-start = ((), (), s32[]{:S(2)}) async-start(), calls=%async_computation.3 | async-start | bytes 2129920 | tf_op jit(solution)/shard_map/reduce_scatter | solution.py:43
  373.8 0.8 copy-start.3
  376.7 2.4 copy-start.4
  376.7 2.4 copy-start.13
  379.1 162.8 %copy-start.11 = (f32[512]{0:T(512)S(1)}, f32[512]{0:T(512)}, u32[]{:S(2)}) copy-start(f32[512]{0:T(512)} %param.14) | copy-start | bytes 6148
  379.1 162.8 %copy-start.12 = (f32[512]{0:T(512)S(1)}, f32[512]{0:T(512)}, u32[]{:S(2)}) copy-start(f32[512]{0:T(512)} %param.13) | copy-start | bytes 6148
  379.1 162.8 %copy-start.9 = (f32[1024]{0:T(1024)S(1)}, f32[1024]{0:T(1024)}, u32[]{:S(2)}) copy-start(f32[1024]{0:T(1024)} %param.15) | copy-start | bytes 12292
  379.1 162.8 %copy-start.10 = (f32[1024]{0:T(1024)S(1)}, f32[1024]{0:T(1024)}, u32[]{:S(2)}) copy-start(f32[1024]{0:T(1024)} %param.12) | copy-start | bytes 12292
  541.9 1.6 copy-start.1
  541.9 103.9 %copy-start.8 = (f32[512]{0:T(512)}, f32[512]{0:T(512)S(1)}, u32[]{:S(2)}) copy-start(f32[512]{0:T(512)S(1)} %get-tuple-element.29) | copy-start | bytes 6148
  541.9 107.6 %copy-start.7 = (f32[512]{0:T(512)}, f32[512]{0:T(512)S(1)}, u32[]{:S(2)}) copy-start(f32[512]{0:T(512)S(1)} %get-tuple-element.28) | copy-start | bytes 6148
  542.0 103.8 %copy-start.6 = (f32[1024]{0:T(1024)}, f32[1024]{0:T(1024)S(1)}, u32[]{:S(2)}) copy-start(f32[1024]{0:T(1024)S(1)} %get-tuple-element.31) | copy-start | bytes 12292
  542.0 107.6 %copy-start.5 = (f32[1024]{0:T(1024)}, f32[1024]{0:T(1024)S(1)}, u32[]{:S(2)}) copy-start(f32[1024]{0:T(1024)S(1)} %get-tuple-element.30) | copy-start | bytes 12292
  647.1 2.4 copy-start.2
Sparse Core Ops, SparseCore 0:
  11.0 134.7 all-gather.2
  148.7 135.0 all-gather.4
  286.8 85.0 all-reduce.5
  376.8 684.5 reduce-scatter.1
where the time goes:
time: 1080 us; the launch traced here: 1070 us
  waiting for transfers between devices  769 us (71%)
  blocking collectives  260 us (24%)
  between operations  15.3 us (1%)
  matrix products  12.7 us (1%)
    reduce_scatter x1, waiting for transfers between devices, per_device(): lax.psum_scatter(lax.dot_general(hidden_grad, w_in, (((1,), (1,)), ((), (...  411 us
    all_gather x1, waiting for transfers between devices, per_device(): lax.all_gather(out_grad, 'mp', axis=0, tiled=True)  137 us
    all_gather x1, waiting for transfers between devices, per_device(): lax.all_gather(inputs, 'mp', axis=0, tiled=True)  135 us
    psum x1, blocking collectives, per_device(): lax.psum((jnp.sum(square_in, axis=1), jnp.sum(square_out, axis=0)), 'mp')  119 us
    psum x1, blocking collectives, per_device(): lax.psum((jnp.sum(step_in * step_in), jnp.sum(step_out * step_out)), ('mp...  99.4 us
    psum x1, waiting for transfers between devices, per_device(): preact, upstream = lax.psum((pre_local, up_local), 'narrow')  85.1 us
    psum x1, blocking collectives, per_device(): lax.psum((jnp.sum(square_in, axis=0), jnp.sum(square_out, axis=1)), 'narr...  41.9 us
  transfers between devices with their start and end apart: 4, of which 4 were waited for; matrix products, arithmetic and copies ran while one was open for 1% of the time, Pallas kernels for 0%

commit v1 on v0

v1 whole, which is shorter than its diff:
```python
import functools

import jax
import jax.numpy as jnp
from jax import lax
from jax.experimental import pallas as pl
from jax.experimental.pallas import tpu as pltpu
from jax.sharding import PartitionSpec as P

D = 8192
FF = 32768
DECAY = 0.8
EPS = 1e-06
CLIP = 0.01

NY, NZ, NX = 4, 16, 4
F32, BF16 = jnp.float32, jnp.bfloat16
MESH = pl.DeviceIdType.MESH
EXACT = lax.Precision.HIGHEST


def dot(a, b, dims, precision=None):
    return lax.dot_general(
        a, b, ((dims[0], dims[1]), ((), ())), precision=precision, preferred_element_type=F32
    )


def fold_lanes(row, parts):
    return jnp.concatenate([row[:, k * 128 : (k + 1) * 128] for k in range(parts)], axis=0)


def unfold_lanes(block, start, parts):
    return jnp.concatenate([block[start + k : start + k + 1, :] for k in range(parts)], axis=1)


def lane_fold(q):
    out = q[:, 0:128]
    for k in range(1, q.shape[1] // 128):
        out = out + q[:, k * 128 : (k + 1) * 128]
    return out


def kernel(
    x_ref, dy_ref, win_ref, wout_ref, rin_ref, cin_ref, rout_ref, cout_ref,
    ig_ref, gin_ref, gout_ref, rin_new, cin_new, rout_new, cout_new, den_ref,
    ga, xs, ds, part, cx, own, sx, xr, hh,
    ys, yr, zs, zr,
    rp_in, rp_out, cs_in, cs_out,
    my, mz, nb, nn, ny, nz,
    yg_s, yg_r, zg_s, zg_r, cx_s, cx_r, xr_s, xr_r, xg_s, xg_r, cg_s, cg_r,
    yi_s, yi_r, zi_s, zi_r, my_s, my_r, mz_s, mz_r, nb_s, nb_r, nn_s, nn_r,
    ny_s, ny_r, nz_s, nz_r,
):
    mp = lax.axis_index("mp")
    nar = lax.axis_index("narrow")
    y, z = mp // NZ, lax.rem(mp, NZ)
    x, c = nar // 2, lax.rem(nar, 2)

    def at_y(d):
        return (lax.rem(y + d, NY) * NZ + z, nar)

    def at_z(d):
        return (y * NZ + lax.rem(z + d, NZ), nar)

    def at_x(d):
        return (mp, lax.rem(x + d, NX) * 2 + c)

    def at_n(d):
        return (mp, lax.rem(nar + d, 8))

    other = (mp, x * 2 + 1 - c)

    def remote(src, dst, ssem, rsem, dev):
        return pltpu.make_async_remote_copy(
            src_ref=src, dst_ref=dst, send_sem=ssem, recv_sem=rsem,
            device_id=dev, device_id_type=MESH,
        )

    barrier = pltpu.get_barrier_semaphore()

    @pl.loop(1, NZ)
    def _(d):
        pl.semaphore_signal(barrier, inc=1, device_id=at_z(d), device_id_type=MESH)

    for d in range(1, NY):
        pl.semaphore_signal(barrier, inc=1, device_id=at_y(d), device_id_type=MESH)
    for d in range(1, 8):
        pl.semaphore_signal(barrier, inc=1, device_id=at_n(d), device_id_type=MESH)

    ga[z, y] = jnp.concatenate(
        [x_ref[...].astype(F32), dy_ref[...].astype(F32)], axis=0
    ).astype(BF16)
    pl.semaphore_wait(barrier, (NZ - 1) + (NY - 1) + 7)

    def y_copy(d):
        return remote(ga.at[z, y], ga.at[z, y], yg_s.at[d], yg_r.at[d], at_y(d))

    def z_copy(way, s, k):
        row = lax.rem(z + (NZ - s if way == 0 else s), NZ)
        col = lax.rem(y + NY - k, NY)
        return remote(
            ga.at[row, col], ga.at[row, col], zg_s.at[way, s, k], zg_r.at[way, s, k],
            at_z(1 if way == 0 else NZ - 1),
        )

    def rows_of(slab):
        block = slab.astype(F32)
        return (
            block[:, 0:8, :].reshape(32, 1024).astype(BF16),
            block[:, 8:16, :].reshape(32, 1024).astype(BF16),
        )

    def work(cells):
        got = [rows_of(ga[cell]) for cell in cells]
        xb = jnp.concatenate([g[0] for g in got], axis=0)
        db = jnp.concatenate([g[1] for g in got], axis=0)
        pre = dot(xb, win_ref[...], ((1,), (0,)))
        up = dot(db, wout_ref[...], ((1,), (1,)))
        for k, cell in enumerate(cells):
            rows = pl.ds(pl.multiple_of(cell * 32, 32), 32)
            xs[rows, :] = got[k][0]
            ds[rows, :] = got[k][1]
            half = cell // 8
            inner = pl.ds(pl.multiple_of(lax.rem(cell, 8) * 32, 32), 32)
            part[half, 0, inner, :] = pre[k * 32 : (k + 1) * 32]
            part[half, 1, inner, :] = up[k * 32 : (k + 1) * 32]

    for d in range(1, NY):
        y_copy(d).start()
    for way in range(2):
        z_copy(way, 0, 0).start()
    for k in range(1, NY):
        y_copy(k).wait_recv()
        for way in range(2):
            z_copy(way, 0, k).start()
    work([z])

    @pl.loop(1, 7)
    def _(s):
        for k in range(NY):
            for way in range(2):
                z_copy(way, s - 1, k).wait_recv()
                z_copy(way, s, k).start()
        work([lax.rem(z + NZ - s, NZ), lax.rem(z + s, NZ)])

    for k in range(NY):
        for way in range(2):
            z_copy(way, 6, k).wait_recv()
            if (k < 2) == (way == 0):
                z_copy(way, 7, k).start()
    work([lax.rem(z + NZ - 7, NZ), lax.rem(z + 7, NZ)])
    for k in range(NY):
        z_copy(0 if k < 2 else 1, 7, k).wait_recv()
    work([lax.rem(z + 8, NZ)])

    core_copy = remote(part.at[1 - c], cx, cx_s, cx_r, other)
    core_copy.start()
    core_copy.wait_recv()

    def piece(i):
        rows = pl.ds(pl.multiple_of(i * 64, 64), 64)
        return part[c, :, rows, :] + cx[:, rows, :]

    def x_copy(d):
        to = lax.rem(x + d, NX)
        return remote(sx.at[to], xr.at[x], xr_s.at[d], xr_r.at[d], at_x(d))

    for d in (2, 1, 3):
        to = lax.rem(x + d, NX)
        sx[to] = piece(to).astype(BF16)
        x_copy(d).start()
    own[...] = piece(x)
    for d in (1, 3, 2):
        x_copy(d).wait_recv()
        own[...] += xr[lax.rem(x + NX - d, NX)].astype(F32)
    pre, up = own[0], own[1]
    sig = 1.0 / (1.0 + jnp.exp(-pre))
    slot = c * NX + x
    hh[0, slot] = (pre * sig).astype(BF16)
    hh[1, slot] = (up * (sig * (1.0 + pre * (1.0 - sig)))).astype(BF16)

    def g_copy(d):
        return remote(hh.at[:, slot], hh.at[:, slot], xg_s.at[d], xg_r.at[d], at_x(d))

    def c_copy(d):
        mine = c * NX + lax.rem(x + NX - d, NX)
        return remote(hh.at[:, mine], hh.at[:, mine], cg_s.at[d], cg_r.at[d], other)

    for d in (2, 1, 3):
        g_copy(d).start()
    c_copy(0).start()
    for d in (1, 3, 2):
        g_copy(d).wait_recv()
        c_copy(d).start()
    for d in (0, 1, 3, 2):
        c_copy(d).wait_recv()

    rp_out[...] = jnp.zeros_like(rp_out)
    cs_in[...] = jnp.zeros_like(cs_in)

    @pl.loop(0, 4)
    def _(j):
        cols = pl.ds(pl.multiple_of(j * 256, 256), 256)
        g = dot(hh[0].reshape(512, 512), ds[:, cols], ((0,), (0,)))
        gout_ref[:, cols] = g
        q = g * g
        cs_out[:, cols] = jnp.sum(q, axis=0, keepdims=True)
        rp_out[...] += lane_fold(q)
        g = dot(xs[:, cols], hh[1].reshape(512, 512), ((0,), (0,)))
        gin_ref[cols, :] = g
        q = g * g
        cs_in[...] += jnp.sum(q, axis=0, keepdims=True)
        rp_in[cols, :] = lane_fold(q)

    ones = jnp.ones((8, 128), F32)
    row_sums_in = dot(ones, rp_in[...], ((1,), (1,)), EXACT)[0:1]
    row_sums_out = dot(ones, rp_out[...], ((1,), (1,)), EXACT)[0:1]
    my[y] = jnp.concatenate([fold_lanes(row_sums_in, 8), fold_lanes(cs_out[...], 8)], axis=0)
    nb[nar] = jnp.concatenate([fold_lanes(cs_in[...], 4), fold_lanes(row_sums_out, 4)], axis=0)

    def my_copy(d):
        return remote(my.at[y], my.at[y], my_s.at[d], my_r.at[d], at_y(d))

    def nb_copy(d):
        return remote(nb.at[nar], nb.at[nar], nb_s.at[d], nb_r.at[d], at_n(d))

    for d in range(1, NY):
        my_copy(d).start()
    for d in range(1, 8):
        nb_copy(d).start()

    @pl.loop(0, 4)
    def _(j):
        h = hh[1, pl.ds(j * 2, 2)].reshape(128, 512)
        p = dot(h, win_ref[...], ((1,), (1,)))
        p = jnp.concatenate([p[:, 0:512].reshape(16, 8, 512), p[:, 512:1024].reshape(16, 8, 512)], axis=1)
        p = p.astype(BF16).reshape(4, 4, 16, 512)
        for k in range(NY):
            ys[k, pl.ds(j * 4, 4)] = p[:, k]

    def yi_copy(d):
        return remote(ys.at[lax.rem(y + d, NY)], yr.at[y], yi_s.at[d], yi_r.at[d], at_y(d))

    for d in (2, 1, 3):
        yi_copy(d).start()

    for d in range(1, NY):
        my_copy(d).wait_recv()
    mz[z] = (my[0] + my[1]) + (my[2] + my[3])

    def mz_copy(d):
        return remote(mz.at[z], mz.at[z], mz_s.at[d], mz_r.at[d], at_z(d))

    @pl.loop(1, NZ)
    def _(d):
        mz_copy(d).start()

    for d in range(1, 8):
        nb_copy(d).wait_recv()
    n_sum = nb[0]
    for k in range(1, 8):
        n_sum = n_sum + nb[k]
    cin_new[...] = DECAY * cin_ref[...] + (1.0 - DECAY) * (unfold_lanes(n_sum, 0, 4) / D + EPS)
    rout_new[...] = DECAY * rout_ref[...] + (1.0 - DECAY) * (unfold_lanes(n_sum, 4, 4) / D + EPS)

    yr[y] = ys[y]
    for d in (1, 3, 2):
        yi_copy(d).wait_recv()

    def zi_copy(d):
        to = lax.rem(z + d, NZ)
        return remote(zs.at[to], zr.at[z], zi_s.at[d], zi_r.at[d], at_z(d))

    @pl.loop(0, NZ)
    def _(k):
        t = (yr[0, k].astype(F32) + yr[1, k].astype(F32)) + (
            yr[2, k].astype(F32) + yr[3, k].astype(F32)
        )
        zs[k] = t.astype(BF16)

    @pl.loop(1, NZ)
    def _(d):
        zi_copy(d).start()

    zr[z] = zs[z]

    @pl.loop(1, NZ)
    def _(d):
        mz_copy(d).wait_recv()

    m_sum = mz[0]
    for k in range(1, NZ):
        m_sum = m_sum + mz[k]
    rin_new[...] = DECAY * rin_ref[...] + (1.0 - DECAY) * (unfold_lanes(m_sum, 0, 8) / FF + EPS)
    cout_new[...] = DECAY * cout_ref[...] + (1.0 - DECAY) * (unfold_lanes(m_sum, 8, 8) / FF + EPS)

    rp_out[...] = jnp.zeros_like(rp_out)
    inv_cin = 1.0 / cin_new[...]

    @pl.loop(0, 4)
    def _(j):
        cols = pl.ds(pl.multiple_of(j * 256, 256), 256)
        g = gout_ref[:, cols]
        rp_out[...] += lane_fold(g * g * (1.0 / cout_new[:, cols]))
        g = gin_ref[cols, :]
        rp_in[cols, :] = lane_fold(g * g * inv_cin)

    inv_rin = jnp.broadcast_to(1.0 / rin_new[...], (8, 1024))
    inv_rout = jnp.broadcast_to(1.0 / rout_new[...], (8, 512))
    n_in = dot(inv_rin, rp_in[...], ((1,), (0,)), EXACT)
    n_out = dot(inv_rout, rp_out[...], ((1,), (0,)), EXACT)
    which = lax.broadcasted_iota(jnp.int32, (8, 128), 0)
    nn[nar] = jnp.where(which < 4, n_in, n_out)

    def nn_copy(d):
        return remote(nn.at[nar], nn.at[nar], nn_s.at[d], nn_r.at[d], at_n(d))

    def ny_copy(d):
        return remote(ny.at[y], ny.at[y], ny_s.at[d], ny_r.at[d], at_y(d))

    def nz_copy(d):
        return remote(nz.at[z], nz.at[z], nz_s.at[d], nz_r.at[d], at_z(d))

    for d in range(1, 8):
        nn_copy(d).start()
    for d in range(1, 8):
        nn_copy(d).wait_recv()
    t = nn[0]
    for k in range(1, 8):
        t = t + nn[k]
    ny[y] = t
    for d in range(1, NY):
        ny_copy(d).start()
    for d in range(1, NY):
        ny_copy(d).wait_recv()
    nz[z] = (ny[0] + ny[1]) + (ny[2] + ny[3])

    @pl.loop(1, NZ)
    def _(d):
        nz_copy(d).start()

    @pl.loop(1, NZ)
    def _(d):
        zi_copy(d).wait_recv()

    t = zr[0].astype(F32)
    for k in range(1, NZ):
        t = t + zr[k].astype(F32)
    ig_ref[...] = jnp.concatenate([t[0:8], t[8:16]], axis=1).astype(BF16)

    @pl.loop(1, NZ)
    def _(d):
        nz_copy(d).wait_recv()

    t = nz[0]
    for k in range(1, NZ):
        t = t + nz[k]
    total = jnp.sum(t, axis=1, keepdims=True)
    den_ref[...] = jnp.broadcast_to(
        jnp.maximum(CLIP, jnp.sqrt(total / (float(D) * float(FF)))), (8, 128)
    )

    for d in range(1, NY):
        y_copy(d).wait_send()
        x_copy(d).wait_send()
        g_copy(d).wait_send()
        my_copy(d).wait_send()
        yi_copy(d).wait_send()
        ny_copy(d).wait_send()
    core_copy.wait_send()
    for d in range(NX):
        c_copy(d).wait_send()
    for d in range(1, 8):
        nb_copy(d).wait_send()
        nn_copy(d).wait_send()

    @pl.loop(0, 7)
    def _(s):
        for k in range(NY):
            for way in range(2):
                z_copy(way, s, k).wait_send()

    for k in range(NY):
        z_copy(0 if k < 2 else 1, 7, k).wait_send()

    @pl.loop(1, NZ)
    def _(d):
        mz_copy(d).wait_send()
        zi_copy(d).wait_send()
        nz_copy(d).wait_send()


def step(*args):
    dma = pltpu.SemaphoreType.DMA
    vmem = pltpu.VMEM
    shape = jax.ShapeDtypeStruct
    outs = (
        shape((8, 1024), BF16), shape((1024, 512), F32), shape((512, 1024), F32),
        shape((1, 1024), F32), shape((1, 512), F32), shape((1, 512), F32), shape((1, 1024), F32),
        shape((8, 128), F32),
    )
    scratch = [
        vmem((NZ, NY, 16, 1024), BF16), vmem((512, 1024), BF16), vmem((512, 1024), BF16),
        vmem((2, 2, 256, 512), F32), vmem((2, 256, 512), F32), vmem((2, 64, 512), F32),
        vmem((NX, 2, 64, 512), BF16), vmem((NX, 2, 64, 512), BF16), vmem((2, 8, 64, 512), BF16),
        vmem((NY, NZ, 16, 512), BF16), vmem((NY, NZ, 16, 512), BF16),
        vmem((NZ, 16, 512), BF16), vmem((NZ, 16, 512), BF16),
        vmem((1024, 128), F32), vmem((512, 128), F32), vmem((1, 512), F32), vmem((1, 1024), F32),
        vmem((NY, 16, 128), F32), vmem((NZ, 16, 128), F32), vmem((8, 8, 128), F32),
        vmem((8, 8, 128), F32), vmem((NY, 8, 128), F32), vmem((NZ, 8, 128), F32),
        dma((NY,)), dma((NY,)), dma((2, 8, NY)), dma((2, 8, NY)), dma, dma,
        dma((NX,)), dma((NX,)), dma((NX,)), dma((NX,)), dma((NX,)), dma((NX,)),
        dma((NY,)), dma((NY,)), dma((NZ,)), dma((NZ,)), dma((NY,)), dma((NY,)),
        dma((NZ,)), dma((NZ,)), dma((8,)), dma((8,)), dma((8,)), dma((8,)),
        dma((NY,)), dma((NY,)), dma((NZ,)), dma((NZ,)),
    ]
    return pl.pallas_call(
        kernel,
        out_shape=outs,
        in_specs=[pl.BlockSpec(memory_space=pltpu.VMEM)] * 8,
        out_specs=[pl.BlockSpec(memory_space=pltpu.VMEM)] * 8,
        scratch_shapes=scratch,
        compiler_params=pltpu.CompilerParams(
            collective_id=1, has_side_effects=True, vmem_limit_bytes=56 * 2**20
        ),
        cost_estimate=pl.CostEstimate(
            flops=2700000000, bytes_accessed=8 * 2**20, transcendentals=100000
        ),
    )(*args)


def per_device(inputs, out_grad, w_in, w_out, row_in, col_in, row_out, col_out):
    line = lambda v: v.reshape(1, -1)
    ig, gin, gout, rin, cin, rout, cout, den = step(
        inputs, out_grad, w_in, w_out, line(row_in), line(col_in), line(row_out), line(col_out)
    )
    rin, cin, rout, cout = rin[0], cin[0], rout[0], cout[0]
    update_in = (gin * lax.rsqrt(rin[:, None] * cin[None, :]) / den[0, 0]).astype(BF16)
    update_out = (gout * lax.rsqrt(rout[:, None] * cout[None, :]) / den[4, 0]).astype(BF16)
    return (ig, update_in, update_out, rin, cin, rout, cout)


def solution(mesh):
    placed = (
        P("mp", "narrow"),
        P("mp", "narrow"),
        P("narrow", "mp"),
        P("mp", "narrow"),
        P("narrow"),
        P("mp"),
        P("mp"),
        P("narrow"),
    )
    return jax.shard_map(
        per_device,
        mesh=mesh,
        in_specs=placed,
        out_specs=(
            P("mp", "narrow"),
            P("narrow", "mp"),
            P("mp", "narrow"),
            P("narrow"),
            P("mp"),
            P("mp"),
            P("narrow"),
        ),
        check_vma=False,
    )
```

time: 1080 us -> 121 us (0.11)
  waiting for transfers between devices: 769 us -> 0 us
  blocking collectives: 260 us -> 0 us
  Pallas kernels: 0 us -> 109 us
  between operations: 15.3 us -> 0.7 us
  matrix products: 12.7 us -> 0 us
    reduce_scatter x1 -> x0, waiting for transfers between devices: 411 us -> none  [per_device(): lax.psum_scatter(lax.dot_general(hidden_grad, w_in, (((1,), (1,)), ((), (...]
    all_gather x2 -> x0, waiting for transfers between devices: 272 us -> none  [the longest x1 137 us: per_device(): lax.all_gather(out_grad, 'mp', axis=0, tiled=True)]
    psum x3 -> x0, blocking collectives: 260 us -> none  [the longest x1 119 us: per_device(): lax.psum((jnp.sum(square_in, axis=1), jnp.sum(square_out, axis=0)), 'mp')]
    pallas_call x0 -> x1, Pallas kernels: none -> 109 us  [step(): pl.pallas_call(kernel, out_shape=outs, in_specs=[pl.BlockSpec(memory_spac...]
    psum x1 -> x0, waiting for transfers between devices: 85.1 us -> none  [per_device(): preact, upstream = lax.psum((pre_local, up_local), 'narrow')]
    dot_general x5 -> x0, matrix products: 12.7 us -> none  [the longest x1 3.25 us: per_device(): lax.dot_general(dy_all, w_out, (((1,), (1,)), ((), ())), preferred_elemen...]
  transfers between devices with their start and end apart: 4 -> 0, of which waited for: 4 -> 0; matrix products, arithmetic and copies ran while one was open for 1% -> 0% of each run, Pallas kernels for 0% -> 0%
where the time goes in v1:
time: 121 us; the launch traced here: 119 us
  Pallas kernels  109 us (90%)
  other arithmetic  5.59 us (5%)
  local copies, waits for them, and re-layouts  4.31 us (4%)
    pallas_call x1, Pallas kernels, step(): pl.pallas_call(kernel, out_shape=outs, in_specs=[pl.BlockSpec(memory_spac...  109 us
    convert_element_type x1, other arithmetic, per_device(): (gout * lax.rsqrt(rout[:, None] * cout[None, :]) / den[4, 0]).astype(BF16)  3.59 us
    unnamed x17, local copies, waits for them, and re-layouts  2.97 us

profile of v1, /device:TPU:1, one launch (start us, length us, event | category | flops | bytes accessed | tf_op | source)
XLA Modules:
  0.0 119.2 jit_solution(18077804956175699459)
XLA Ops:
  0.6 108.6 %shard_map.135 = (bf16[8,1024]{1,0:T(8,128)(2,1)}, f32[1024,512]{1,0:T(8,128)}, f32[512,1024]{1,0:T(8,128)}, f32[1,1024]{1,0:T(1,128)}, f32[1,512]{1,0:T(1,128)}...) custom-call(bf16[8,1024]{1,0:T(8,128)(2,1)} %x_ref.1, bf16[8,1024]{1,0:T(8,128)(2,1)} %dy_ref.1, ...), custom_call_target="tpu_custom_call" | custom-call | flops 2700000000 | bytes 8388608 | tf_op jit(solution)/shard_map/pallas_call | solution.py:417
  109.2 0.0 copy-start
  109.2 0.0 copy-start.2
  109.2 0.0 copy-start.5
  109.3 1.3 %fusion = (f32[1,1]{1,0:T(1,128)}, f32[1,1]{1,0:T(1,128)}) fusion(f32[8,128]{1,0:T(8,128)} %get-tuple-element.19), kind=kLoop, calls=%fused_computation.2 | loop fusion | bytes 16 | tf_op jit(solution)/shard_map/slice | solution.py:439
  110.6 3.6 %divide_convert_fusion = bf16[512,1024]{1,0:T(8,128)(2,1)} fusion(f32[512,1024]{1,0:T(8,128)} %get-tuple-element.20, f32[]{:T(128)} %bitcast.9, f32[1024]{0:T(1024)} %bitcast.10, f32[512]{0:T(512)} %bitcast.14), kind=kLoop, calls=%fused_computation | loop fusion | flops 2097152 | bytes 3151876 | tf_op jit(solution)/shard_map/convert_element_type | solution.py:439
  114.2 0.0 copy-done
  114.2 0.0 copy-done.2
  114.2 0.0 copy-done.5
  114.2 0.0 copy-start.3
  114.2 0.0 copy-start.4
  114.2 0.0 copy-start.1
  114.2 2.0 %divide_convert_fusion.1 = bf16[1024,512]{1,0:T(8,128)(2,1)} fusion(f32[1024,512]{1,0:T(8,128)S(1)} %copy-done, f32[]{:T(128)} %bitcast.6, f32[512]{0:T(512)S(1)} %bitcast.16, f32[1024]{0:T(1024)S(1)} %bitcast.12), kind=kLoop, calls=%fused_computation.1 | loop fusion | flops 2097152 | bytes 3151876 | tf_op jit(solution)/shard_map/convert_element_type | solution.py:438
  116.2 0.0 copy-done.3
  116.2 0.6 copy.20
  116.8 0.6 copy.21
  117.4 0.6 copy.22
  118.0 0.0 copy-done.4
  118.0 0.6 copy.23
  118.6 0.0 copy-done.1
  118.6 0.6 copy.24
Async XLA Ops:
  109.2 5.0 %copy-start = (f32[1024,512]{1,0:T(8,128)S(1)}, f32[1024,512]{1,0:T(8,128)}, u32[]{:S(2)}) copy-start(f32[1024,512]{1,0:T(8,128)} %get-tuple-element.16) | copy-start | bytes 6291460
  109.2 5.0 %copy-start.2 = (f32[1,1024]{1,0:T(1,128)S(1)}, f32[1,1024]{1,0:T(1,128)}, u32[]{:S(2)}) copy-start(f32[1,1024]{1,0:T(1,128)} %get-tuple-element.17) | copy-start | bytes 12292
  109.2 4.9 %copy-start.5 = (f32[1,512]{1,0:T(1,128)S(1)}, f32[1,512]{1,0:T(1,128)}, u32[]{:S(2)}) copy-start(f32[1,512]{1,0:T(1,128)} %get-tuple-element.18) | copy-start | bytes 6148
  114.2 2.0 %copy-start.3 = (bf16[8,1024]{1,0:T(8,128)(2,1)S(1)}, bf16[8,1024]{1,0:T(8,128)(2,1)}, u32[]{:S(2)}) copy-start(bf16[8,1024]{1,0:T(8,128)(2,1)} %get-tuple-element.32) | copy-start | bytes 49156
  114.2 3.8 %copy-start.4 = (f32[1,512]{1,0:T(1,128)S(1)}, f32[1,512]{1,0:T(1,128)}, u32[]{:S(2)}) copy-start(f32[1,512]{1,0:T(1,128)} %get-tuple-element.21) | copy-start | bytes 6148
  114.2 4.4 %copy-start.1 = (f32[1,1024]{1,0:T(1,128)S(1)}, f32[1,1024]{1,0:T(1,128)}, u32[]{:S(2)}) copy-start(f32[1,1024]{1,0:T(1,128)} %get-tuple-element.22) | copy-start | bytes 12292

commit v2 on v1

v2 whole, which is shorter than its diff:
```python
import functools

import jax
import jax.numpy as jnp
from jax import lax
from jax.experimental import pallas as pl
from jax.experimental.pallas import tpu as pltpu
from jax.sharding import PartitionSpec as P

D = 8192
FF = 32768
DECAY = 0.8
EPS = 1e-06
CLIP = 0.01

NY, NZ, NX = 4, 16, 4
F32, BF16 = jnp.float32, jnp.bfloat16
MESH = pl.DeviceIdType.MESH
EXACT = lax.Precision.HIGHEST
LAG = (1, 3, 5, 6, 8)


def dot(a, b, dims, precision=None):
    return lax.dot_general(
        a, b, ((dims[0], dims[1]), ((), ())), precision=precision, preferred_element_type=F32
    )


def fold_lanes(row, parts):
    return jnp.concatenate([row[:, k * 128 : (k + 1) * 128] for k in range(parts)], axis=0)


def unfold_lanes(block, start, parts):
    return jnp.concatenate([block[start + k : start + k + 1, :] for k in range(parts)], axis=1)


def lane_fold(q):
    out = q[:, 0:128]
    for k in range(1, q.shape[1] // 128):
        out = out + q[:, k * 128 : (k + 1) * 128]
    return out


def columns_of(row):
    return jnp.transpose(jnp.broadcast_to(row, (128, row.shape[1])))


def kernel(
    x_ref, dy_ref, win_hbm, wout_hbm, rin_ref, cin_ref, rout_ref, cout_ref,
    ig_ref, gin_hbm, gout_hbm, rin_new, cin_new, rout_new, cout_new, den_ref,
    win_ref, wout_ref, gin_ref, gout_ref,
    ga, xs, ds, acts, hgs, keep, give, cx, tot, sx, xr, hh,
    ys, yr, zs, zr,
    rp_in, rp_out, cs_in, cs_out,
    my, mz, ty, tz, nb, nn,
    w_sem, o_sem,
    yg_s, yg_r, zg_s, zg_r, cx_s, cx_r, xr_s, xr_r, xg_s, xg_r, cg_s, cg_r,
    yi_s, yi_r, zi_s, zi_r, my_s, my_r, mz_s, mz_r, ty_s, ty_r, tz_s, tz_r,
    nb_s, nb_r, nn_s, nn_r,
):
    mp = lax.axis_index("mp")
    nar = lax.axis_index("narrow")
    y, z = mp // NZ, lax.rem(mp, NZ)
    x, c = nar // 2, lax.rem(nar, 2)

    def at_y(d):
        return (lax.rem(y + d, NY) * NZ + z, nar)

    def at_z(d):
        return (y * NZ + lax.rem(z + d, NZ), nar)

    def at_x(d):
        return (mp, lax.rem(x + d, NX) * 2 + c)

    def at_n(d):
        return (mp, lax.rem(nar + d, 8))

    other = (mp, x * 2 + 1 - c)

    def remote(src, dst, ssem, rsem, dev):
        return pltpu.make_async_remote_copy(
            src_ref=src, dst_ref=dst, send_sem=ssem, recv_sem=rsem,
            device_id=dev, device_id_type=MESH,
        )

    barrier = pltpu.get_barrier_semaphore()
    greet = [at_y(1), at_y(2), at_y(3), at_z(1), at_z(NZ - 1), at_x(1), at_x(2), at_x(3), other]
    for dev in greet:
        pl.semaphore_signal(barrier, inc=1, device_id=dev, device_id_type=MESH)

    load_in = pltpu.make_async_copy(win_hbm, win_ref, w_sem.at[0])
    load_out = pltpu.make_async_copy(wout_hbm, wout_ref, w_sem.at[1])
    load_in.start()
    load_out.start()
    ga[z, y] = jnp.concatenate(
        [x_ref[...].astype(F32), dy_ref[...].astype(F32)], axis=0
    ).astype(BF16)
    pl.semaphore_wait(barrier, len(greet))

    def y_copy(d):
        return remote(ga.at[z, y], ga.at[z, y], yg_s.at[d], yg_r.at[d], at_y(d))

    def z_copy(way, s, k):
        row = lax.rem(z + (NZ - s if way == 0 else s), NZ)
        col = lax.rem(y + NY - k, NY)
        return remote(
            ga.at[row, col], ga.at[row, col], zg_s.at[way, s, k], zg_r.at[way, s, k],
            at_z(1 if way == 0 else NZ - 1),
        )

    def pair(s):
        first = lax.rem(z + NZ - s, NZ)
        second = lax.rem(z + lax.rem(s, 8), NZ)
        return jnp.where(c == 0, first, second), jnp.where(c == 0, second, first)

    def rows32(cell):
        return pl.ds(pl.multiple_of(cell * 32, 32), 32)

    def split16(block, width):
        block = block.astype(F32)
        return (
            block[:, 0:8, :].reshape(32, width).astype(BF16),
            block[:, 8:16, :].reshape(32, width).astype(BF16),
        )

    def cx_copy(s):
        i = s - 1
        return remote(give.at[i], cx.at[i], cx_s.at[i], cx_r.at[i], other)

    def xr_copy(s, d):
        i = s - 1
        to = lax.rem(x + d, NX)
        return remote(sx.at[i, to], xr.at[i, x], xr_s.at[i, d], xr_r.at[i, d], at_x(d))

    def xg_copy(s, d):
        ref = hh.at[pair(s)[0], x]
        return remote(ref, ref, xg_s.at[s - 1, d], xg_r.at[s - 1, d], at_x(d))

    def cg_copy(s, d):
        ref = hh.at[pair(s)[0], lax.rem(x + NX - d, NX)]
        return remote(ref, ref, cg_s.at[s - 1, d], cg_r.at[s - 1, d], other)

    def yi_copy(s, d):
        i = s - 1
        to = lax.rem(y + d, NY)
        return remote(ys.at[i, to], yr.at[i, y], yi_s.at[i, d], yi_r.at[i, d], at_y(d))

    def zi_copy(d):
        to = lax.rem(z + d, NZ)
        return remote(zs.at[to], zr.at[z], zi_s.at[d], zi_r.at[d], at_z(d))

    def project(s):
        cells = pair(s)
        got = [split16(ga[cell], 1024) for cell in cells]
        xb = jnp.concatenate([g[0] for g in got], axis=0)
        db = jnp.concatenate([g[1] for g in got], axis=0)
        pre = dot(xb, win_ref[...], ((1,), (0,)))
        up = dot(db, wout_ref[...], ((1,), (1,)))
        i = s - 1
        keep[i, 0] = pre[0:32]
        keep[i, 1] = up[0:32]
        give[i, 0] = pre[32:64]
        give[i, 1] = up[32:64]
        cx_copy(s).start()
        for g, cell in zip(got, cells):
            xs[rows32(cell), :] = g[0]
            ds[rows32(cell), :] = g[1]

    def spread(s):
        i = s - 1
        cx_copy(s).wait_recv()
        t = keep[i] + cx[i]
        t = jnp.concatenate([t[0].reshape(4, 8, 512), t[1].reshape(4, 8, 512)], axis=1)
        tot[i] = t
        sx[i] = t.astype(BF16)
        for d in (2, 1, 3):
            xr_copy(s, d).start()

    def activate(s):
        i = s - 1
        t = tot[i, x]
        for d in (1, 3, 2):
            xr_copy(s, d).wait_recv()
            t = t + xr[i, lax.rem(x + NX - d, NX)].astype(F32)
        pre, up = t[0:8], t[8:16]
        sig = 1.0 / (1.0 + jnp.exp(-pre))
        hh[pair(s)[0], x] = jnp.concatenate(
            [pre * sig, up * (sig * (1.0 + pre * (1.0 - sig)))], axis=0
        ).astype(BF16)
        for d in (2, 1, 3):
            xg_copy(s, d).start()
        cg_copy(s, 0).start()

    def hand_over(s):
        for d in (1, 3, 2):
            xg_copy(s, d).wait_recv()
            cg_copy(s, d).start()

    def back_project(s):
        for d in (0, 1, 3, 2):
            cg_copy(s, d).wait_recv()
        cells = pair(s)
        got = [split16(hh[cell], 512) for cell in cells]
        p = dot(jnp.concatenate([g[1] for g in got], axis=0), win_ref[...], ((1,), (1,)))
        p = p.reshape(2, 4, 8, 1024)
        p = jnp.concatenate([p[..., 0:512], p[..., 512:1024]], axis=2).astype(BF16)
        for k in range(NY):
            ys[s - 1, k] = p[:, k]
        for d in (2, 1, 3):
            yi_copy(s, d).start()
        for g, cell in zip(got, cells):
            acts[rows32(cell), :] = g[0]
            hgs[rows32(cell), :] = g[1]

    def deliver(s):
        i = s - 1
        yr[i, y] = ys[i, y]
        for d in (1, 3, 2):
            yi_copy(s, d).wait_recv()
        t = (yr[i, 0].astype(F32) + yr[i, 1].astype(F32)) + (
            yr[i, 2].astype(F32) + yr[i, 3].astype(F32)
        )
        for k, cell in enumerate(pair(s)):
            zs[cell] = t[k].astype(BF16)

        zi_copy(NZ - s).start()

        @pl.when(s < 8)
        def _():
            zi_copy(lax.rem(s, NZ)).start()

    for d in (2, 1, 3):
        y_copy(d).start()
    for way in range(2):
        z_copy(way, 0, 0).start()
    for k in (1, 3, 2):
        y_copy(k).wait_recv()
        for way in range(2):
            z_copy(way, 0, k).start()
    load_in.wait()
    load_out.wait()

    @pl.loop(1, 8 + LAG[3] + 1)
    def _(s):
        @pl.when(s < 7)
        def _():
            for k in (0, 1, 3, 2):
                for way in range(2):
                    z_copy(way, s - 1, k).wait_recv()
                    z_copy(way, s, k).start()

        @pl.when(s == 7)
        def _():
            for k in (0, 1, 3, 2):
                for way in range(2):
                    z_copy(way, 6, k).wait_recv()
                    if (k < 2) == (way == 0):
                        z_copy(way, 7, k).start()

        @pl.when(s == 8)
        def _():
            for k in (0, 1, 3, 2):
                z_copy(0 if k < 2 else 1, 7, k).wait_recv()

        def stage(lag, run):
            @pl.when(jnp.logical_and(s > lag, s <= 8 + lag))
            def _():
                run(s - lag)

        stage(LAG[4], deliver)
        stage(LAG[3], back_project)
        stage(LAG[2], hand_over)
        stage(LAG[1], activate)
        stage(LAG[0], spread)

        @pl.when(s <= 8)
        def _():
            project(s)

    rp_out[...] = jnp.zeros_like(rp_out)
    cs_in[...] = jnp.zeros_like(cs_in)

    @pl.loop(0, 4)
    def _(j):
        cols = pl.ds(pl.multiple_of(j * 256, 256), 256)
        g = dot(acts[...], ds[:, cols], ((0,), (0,)))
        gout_ref[:, cols] = g
        q = g * g
        cs_out[:, cols] = jnp.sum(q, axis=0, keepdims=True)
        rp_out[...] += lane_fold(q)
        g = dot(xs[:, cols], hgs[...], ((0,), (0,)))
        gin_ref[cols, :] = g
        q = g * g
        cs_in[...] += jnp.sum(q, axis=0, keepdims=True)
        rp_in[cols, :] = lane_fold(q)

    save_in = pltpu.make_async_copy(gin_ref, gin_hbm, o_sem.at[0])
    save_out = pltpu.make_async_copy(gout_ref, gout_hbm, o_sem.at[1])
    ones = jnp.ones((8, 128), F32)

    def my_copy(d):
        return remote(my.at[y], my.at[y], my_s.at[d], my_r.at[d], at_y(d))

    def mz_copy(d):
        return remote(mz.at[z], mz.at[z], mz_s.at[d], mz_r.at[d], at_z(d))

    def ty_copy(d):
        return remote(ty.at[y], ty.at[y], ty_s.at[d], ty_r.at[d], at_y(d))

    def tz_copy(d):
        return remote(tz.at[z], tz.at[z], tz_s.at[d], tz_r.at[d], at_z(d))

    def nb_copy(d):
        return remote(nb.at[nar], nb.at[nar], nb_s.at[d], nb_r.at[d], at_n(d))

    def nn_copy(d):
        return remote(nn.at[nar], nn.at[nar], nn_s.at[d], nn_r.at[d], at_n(d))

    row_sums_out = dot(ones, rp_out[...], ((1,), (1,)), EXACT)[0:1]
    nb[nar] = jnp.concatenate([fold_lanes(cs_in[...], 4), fold_lanes(row_sums_out, 4)], axis=0)
    for d in range(1, 8):
        nb_copy(d).start()
    row_sums_in = dot(ones, rp_in[...], ((1,), (1,)), EXACT)[0:1]
    my[y] = jnp.concatenate([fold_lanes(row_sums_in, 8), fold_lanes(cs_out[...], 8)], axis=0)
    for d in range(1, NY):
        my_copy(d).start()
    save_in.start()
    save_out.start()

    for s in range(8 + LAG[3] - LAG[4] + 1, 9):
        deliver(s)
    zr[z] = zs[z]

    for d in range(1, 8):
        nb_copy(d).wait_recv()
    n_sum = nb[0]
    for k in range(1, 8):
        n_sum = n_sum + nb[k]
    cin_new[...] = DECAY * cin_ref[...] + (1.0 - DECAY) * (unfold_lanes(n_sum, 0, 4) / D + EPS)
    rout_new[...] = DECAY * rout_ref[...] + (1.0 - DECAY) * (unfold_lanes(n_sum, 4, 4) / D + EPS)

    inv_cin = 1.0 / cin_new[...]
    rp_out[...] = columns_of(1.0 / rout_new[...])

    @pl.loop(0, 4)
    def _(j):
        cols = pl.ds(pl.multiple_of(j * 256, 256), 256)
        g = gout_ref[:, cols]
        q = g * g
        w = rp_out[...]
        q = jnp.concatenate([q[:, 0:128] * w, q[:, 128:256] * w], axis=1)
        cs_out[:, cols] = jnp.sum(q, axis=0, keepdims=True)
        g = gin_ref[cols, :]
        rp_in[cols, :] = lane_fold(g * g * inv_cin)

    t_in = dot(ones, rp_in[...], ((1,), (1,)), EXACT)[0:1]
    ty[y] = jnp.concatenate([fold_lanes(t_in, 8), fold_lanes(cs_out[...], 8)], axis=0)
    for d in range(1, NY):
        ty_copy(d).start()

    for d in range(1, NY):
        my_copy(d).wait_recv()
    mz[z] = (my[0] + my[1]) + (my[2] + my[3])

    @pl.loop(1, NZ)
    def _(d):
        mz_copy(d).start()

    for d in range(1, NY):
        ty_copy(d).wait_recv()
    tz[z] = ((ty[0] + ty[1]) + (ty[2] + ty[3])).astype(BF16)

    @pl.loop(1, NZ)
    def _(d):
        tz_copy(d).start()

    @pl.loop(1, NZ)
    def _(d):
        zi_copy(d).wait_recv()

    t = zr[0].astype(F32)
    for k in range(1, NZ):
        t = t + zr[k].astype(F32)
    ig_ref[...] = jnp.concatenate([t[0:8], t[8:16]], axis=1).astype(BF16)

    @pl.loop(1, NZ)
    def _(d):
        mz_copy(d).wait_recv()

    m_sum = mz[0]
    for k in range(1, NZ):
        m_sum = m_sum + mz[k]
    r_new = DECAY * rin_ref[...] + (1.0 - DECAY) * (unfold_lanes(m_sum, 0, 8) / FF + EPS)
    c_new = DECAY * cout_ref[...] + (1.0 - DECAY) * (unfold_lanes(m_sum, 8, 8) / FF + EPS)
    rin_new[...] = r_new
    cout_new[...] = c_new
    inv_r, inv_c = fold_lanes(1.0 / r_new, 8), fold_lanes(1.0 / c_new, 8)

    @pl.loop(1, NZ)
    def _(d):
        tz_copy(d).wait_recv()

    t = tz[0].astype(F32)
    for k in range(1, NZ):
        t = t + tz[k].astype(F32)
    n_in = jnp.sum(t[0:8] * inv_r, axis=0, keepdims=True)
    n_out = jnp.sum(t[8:16] * inv_c, axis=0, keepdims=True)
    which = lax.broadcasted_iota(jnp.int32, (8, 128), 0)
    nn[nar] = jnp.where(which < 4, n_in, n_out)
    for d in range(1, 8):
        nn_copy(d).start()
    for d in range(1, 8):
        nn_copy(d).wait_recv()
    t = nn[0]
    for k in range(1, 8):
        t = t + nn[k]
    total = jnp.sum(t, axis=1, keepdims=True)
    den_ref[...] = jnp.broadcast_to(
        jnp.maximum(CLIP, jnp.sqrt(total / (float(D) * float(FF)))), (8, 128)
    )

    save_in.wait()
    save_out.wait()
    for d in range(1, NY):
        y_copy(d).wait_send()
        my_copy(d).wait_send()
        ty_copy(d).wait_send()

    @pl.loop(1, 9)
    def _(s):
        cx_copy(s).wait_send()
        cg_copy(s, 0).wait_send()
        for d in range(1, NX):
            xr_copy(s, d).wait_send()
            xg_copy(s, d).wait_send()
            cg_copy(s, d).wait_send()
            yi_copy(s, d).wait_send()

    for d in range(1, 8):
        nb_copy(d).wait_send()
        nn_copy(d).wait_send()

    @pl.loop(0, 7)
    def _(s):
        for k in range(NY):
            for way in range(2):
                z_copy(way, s, k).wait_send()

    for k in range(NY):
        z_copy(0 if k < 2 else 1, 7, k).wait_send()

    @pl.loop(1, NZ)
    def _(d):
        mz_copy(d).wait_send()
        tz_copy(d).wait_send()
        zi_copy(d).wait_send()


VMEM_SPEC = pl.BlockSpec(memory_space=pltpu.VMEM)
ANY_SPEC = pl.BlockSpec(memory_space=pl.ANY)


def step(*args):
    dma = pltpu.SemaphoreType.DMA
    vmem = pltpu.VMEM
    shape = jax.ShapeDtypeStruct
    outs = (
        shape((8, 1024), BF16), shape((1024, 512), F32), shape((512, 1024), F32),
        shape((1, 1024), F32), shape((1, 512), F32), shape((1, 512), F32), shape((1, 1024), F32),
        shape((8, 128), F32),
    )
    scratch = [
        vmem((1024, 512), BF16), vmem((512, 1024), BF16),
        vmem((1024, 512), F32), vmem((512, 1024), F32),
        vmem((NZ, NY, 16, 1024), BF16), vmem((512, 1024), BF16), vmem((512, 1024), BF16),
        vmem((512, 512), BF16), vmem((512, 512), BF16),
        vmem((8, 2, 32, 512), F32), vmem((8, 2, 32, 512), F32), vmem((8, 2, 32, 512), F32),
        vmem((8, NX, 16, 512), F32), vmem((8, NX, 16, 512), BF16), vmem((8, NX, 16, 512), BF16),
        vmem((NZ, NX, 16, 512), BF16),
        vmem((8, NY, 2, 16, 512), BF16), vmem((8, NY, 2, 16, 512), BF16),
        vmem((NZ, 16, 512), BF16), vmem((NZ, 16, 512), BF16),
        vmem((1024, 128), F32), vmem((512, 128), F32), vmem((1, 512), F32), vmem((1, 1024), F32),
        vmem((NY, 16, 128), F32), vmem((NZ, 16, 128), F32),
        vmem((NY, 16, 128), F32), vmem((NZ, 16, 128), BF16),
        vmem((8, 8, 128), F32), vmem((8, 8, 128), F32),
        dma((2,)), dma((2,)),
        dma((NY,)), dma((NY,)), dma((2, 8, NY)), dma((2, 8, NY)), dma((8,)), dma((8,)),
        dma((8, NX)), dma((8, NX)), dma((8, NX)), dma((8, NX)), dma((8, NX)), dma((8, NX)),
        dma((8, NY)), dma((8, NY)), dma((NZ,)), dma((NZ,)),
        dma((NY,)), dma((NY,)), dma((NZ,)), dma((NZ,)),
        dma((NY,)), dma((NY,)), dma((NZ,)), dma((NZ,)),
        dma((8,)), dma((8,)), dma((8,)), dma((8,)),
    ]
    return pl.pallas_call(
        kernel,
        out_shape=outs,
        in_specs=[VMEM_SPEC, VMEM_SPEC, ANY_SPEC, ANY_SPEC] + [VMEM_SPEC] * 4,
        out_specs=[VMEM_SPEC, ANY_SPEC, ANY_SPEC] + [VMEM_SPEC] * 5,
        scratch_shapes=scratch,
        compiler_params=pltpu.CompilerParams(
            collective_id=1, has_side_effects=True, vmem_limit_bytes=56 * 2**20
        ),
        cost_estimate=pl.CostEstimate(
            flops=2700000000, bytes_accessed=8 * 2**20, transcendentals=100000
        ),
    )(*args)


STEPS = 4


def scale_kernel(
    ig_ref, gin_ref, gout_ref, rin_ref, cin_ref, rout_ref, cout_ref, den_ref,
    ig_out, uin_ref, uout_ref, rin_out, cin_out, rout_out, cout_out,
):
    j = pl.program_id(0)

    @pl.when(j == 0)
    def _():
        ig_out[...] = ig_ref[...]
        rin_out[...] = fold_lanes(rin_ref[...], 8)
        cin_out[...] = fold_lanes(cin_ref[...], 4)
        rout_out[...] = fold_lanes(rout_ref[...], 4)
        cout_out[...] = fold_lanes(cout_ref[...], 8)

    def update(g_ref, row, col_ref, den, u_ref):
        r = columns_of(row)
        for k in range(g_ref.shape[1] // 128):
            lanes = slice(k * 128, (k + 1) * 128)
            u_ref[:, lanes] = (
                g_ref[:, lanes] * lax.rsqrt(r * col_ref[:, lanes]) / den
            ).astype(BF16)

    many, few = 1024 // STEPS, 512 // STEPS
    update(
        gin_ref, rin_ref[:, pl.ds(pl.multiple_of(j * many, many), many)], cin_ref,
        den_ref[0:1, :], uin_ref,
    )
    update(
        gout_ref, rout_ref[:, pl.ds(pl.multiple_of(j * few, few), few)], cout_ref,
        den_ref[4:5, :], uout_ref,
    )


def scale(*args):
    shape = jax.ShapeDtypeStruct
    whole = lambda *dims: pl.BlockSpec(dims, lambda j: (0, 0))
    big = lambda *dims: pl.BlockSpec(dims, lambda j: (j, 0))
    return pl.pallas_call(
        scale_kernel,
        grid=(STEPS,),
        in_specs=[
            whole(8, 1024), big(1024 // STEPS, 512), big(512 // STEPS, 1024),
            whole(1, 1024), whole(1, 512), whole(1, 512), whole(1, 1024), whole(8, 128),
        ],
        out_specs=[
            whole(8, 1024), big(1024 // STEPS, 512), big(512 // STEPS, 1024),
            whole(8, 128), whole(4, 128), whole(4, 128), whole(8, 128),
        ],
        out_shape=(
            shape((8, 1024), BF16), shape((1024, 512), BF16), shape((512, 1024), BF16),
            shape((8, 128), F32), shape((4, 128), F32), shape((4, 128), F32), shape((8, 128), F32),
        ),
        compiler_params=pltpu.CompilerParams(vmem_limit_bytes=56 * 2**20),
    )(*args)


def per_device(inputs, out_grad, w_in, w_out, row_in, col_in, row_out, col_out):
    line = lambda v: v.reshape(1, -1)
    whole = step(
        inputs, out_grad, w_in, w_out, line(row_in), line(col_in), line(row_out), line(col_out)
    )
    ig, update_in, update_out, rin, cin, rout, cout = scale(*whole)
    return (
        ig, update_in, update_out,
        rin.reshape(-1), cin.reshape(-1), rout.reshape(-1), cout.reshape(-1),
    )


def solution(mesh):
    placed = (
        P("mp", "narrow"),
        P("mp", "narrow"),
        P("narrow", "mp"),
        P("mp", "narrow"),
        P("narrow"),
        P("mp"),
        P("mp"),
        P("narrow"),
    )
    return jax.shard_map(
        per_device,
        mesh=mesh,
        in_specs=placed,
        out_specs=(
            P("mp", "narrow"),
            P("narrow", "mp"),
            P("mp", "narrow"),
            P("narrow"),
            P("mp"),
            P("mp"),
            P("narrow"),
        ),
        check_vma=False,
    )
```

time: 121 us -> 96.3 us (0.80); the launches traced: 119 us -> 96 us
  Pallas kernels: 109 us -> 95.4 us
  other arithmetic: 5.59 us -> 0 us
  local copies, waits for them, and re-layouts: 4.31 us -> 0 us
    pallas_call x1 -> x2, Pallas kernels: 109 us -> 95.4 us  [the longest x1 90.8 us: step(): pl.pallas_call(kernel, out_shape=outs, in_specs=[VMEM_SPEC, VMEM_SPEC, AN...]
    convert_element_type x2 -> x0, other arithmetic: 5.59 us -> none  [the longest x1 3.59 us: per_device(): (gout * lax.rsqrt(rout[:, None] * cout[None, :]) / den[4, 0]).astype(BF16)]
    unnamed x17 -> x0, local copies, waits for them, and re-layouts: 2.97 us -> none
    slice x1 -> x0, local copies, waits for them, and re-layouts: 1.34 us -> none  [per_device(): den[4, 0]]
where the time goes in v2:
time: 96.3 us; the launch traced here: 96 us
  Pallas kernels  95.4 us (99%)
    pallas_call x1, Pallas kernels, step(): pl.pallas_call(kernel, out_shape=outs, in_specs=[VMEM_SPEC, VMEM_SPEC, AN...  90.8 us
    pallas_call x1, Pallas kernels, scale(): pl.pallas_call(scale_kernel, grid=(STEPS,), in_specs=[whole(8, 1024), big...  4.59 us

profile of v2, /device:TPU:1, one launch (start us, length us, event | category | flops | bytes accessed | tf_op | source)
XLA Modules:
  0.0 96.0 jit_solution(763873288456453502)
XLA Ops:
  0.6 90.8 %shard_map.135 = (bf16[8,1024]{1,0:T(8,128)(2,1)}, f32[1024,512]{1,0:T(8,128)}, f32[512,1024]{1,0:T(8,128)}, f32[1,1024]{1,0:T(1,128)}, f32[1,512]{1,0:T(1,128)}...) custom-call(bf16[8,1024]{1,0:T(8,128)(2,1)} %x_ref.1, bf16[8,1024]{1,0:T(8,128)(2,1)} %dy_ref.1, ...), custom_call_target="tpu_custom_call" | custom-call | flops 2700000000 | bytes 8388608 | tf_op jit(solution)/shard_map/pallas_call | solution.py:494
  91.4 4.6 %shard_map.136 = (bf16[8,1024]{1,0:T(8,128)(2,1)}, bf16[1024,512]{1,0:T(8,128)(2,1)}, bf16[512,1024]{1,0:T(8,128)(2,1)}, f32[8,128]{1,0:T(8,128)}, f32[4,128]{1,...) custom-call(bf16[8,1024]{1,0:T(8,128)(2,1)} %get-tuple-element.22.ig_ref, f32[1024,512]{1,0:T(8,128)} %get-tuple-element.23.gin_ref, ...), custom_call_target="tpu_custom_call" | custom-call | tf_op jit(solution)/shard_map/pallas_call | solution.py:549

commit v3 on v2

--- a/solution.py
+++ b/solution.py
@@ -17,7 +17,8 @@
 F32, BF16 = jnp.float32, jnp.bfloat16
 MESH = pl.DeviceIdType.MESH
 EXACT = lax.Precision.HIGHEST
-LAG = (1, 3, 5, 6, 8)
+LAG = (1, 3, 5, 7)
+FAR_FIRST = (8, 7, 9, 6, 10, 5, 11, 4, 12, 3, 13, 2, 14, 1, 15)
 
 
 def dot(a, b, dims, precision=None):
@@ -46,15 +47,16 @@
 
 
 def kernel(
-    x_ref, dy_ref, win_hbm, wout_hbm, rin_ref, cin_ref, rout_ref, cout_ref,
-    ig_ref, gin_hbm, gout_hbm, rin_new, cin_new, rout_new, cout_new, den_ref,
-    win_ref, wout_ref, gin_ref, gout_ref,
-    ga, xs, ds, acts, hgs, keep, give, cx, tot, sx, xr, hh,
+    x_hbm, dy_hbm, win_hbm, wout_hbm, rin_hbm, cin_hbm, rout_hbm, cout_hbm,
+    ig_hbm, gin_hbm, gout_hbm, vec_hbm,
+    x_ref, dy_ref, win_ref, wout_ref, rin_ref, cin_ref, rout_ref, cout_ref,
+    ig_ref, gin_ref, gout_ref, vec_ref,
+    g1, g2, xs, ds, acts, hgs, keep, give, cx, tot, sx, xr, hh,
     ys, yr, zs, zr,
     rp_in, rp_out, cs_in, cs_out,
     my, mz, ty, tz, nb, nn,
     w_sem, o_sem,
-    yg_s, yg_r, zg_s, zg_r, cx_s, cx_r, xr_s, xr_r, xg_s, xg_r, cg_s, cg_r,
+    yg_s, yg_r, zg_s, zg_r, y2_s, y2_r, z2_s, z2_r, cx_s, cx_r, xr_s, xr_r, xg_s, xg_r,
     yi_s, yi_r, zi_s, zi_r, my_s, my_r, mz_s, mz_r, ty_s, ty_r, tz_s, tz_r,
     nb_s, nb_r, nn_s, nn_r,
 ):
@@ -88,25 +90,43 @@
     for dev in greet:
         pl.semaphore_signal(barrier, inc=1, device_id=dev, device_id_type=MESH)
 
-    load_in = pltpu.make_async_copy(win_hbm, win_ref, w_sem.at[0])
-    load_out = pltpu.make_async_copy(wout_hbm, wout_ref, w_sem.at[1])
-    load_in.start()
-    load_out.start()
-    ga[z, y] = jnp.concatenate(
-        [x_ref[...].astype(F32), dy_ref[...].astype(F32)], axis=0
-    ).astype(BF16)
+    loads = [
+        pltpu.make_async_copy(src, dst, w_sem.at[k])
+        for k, (src, dst) in enumerate((
+            (x_hbm, x_ref), (dy_hbm, dy_ref), (win_hbm, win_ref), (wout_hbm, wout_ref),
+            (rin_hbm, rin_ref), (cin_hbm, cin_ref), (rout_hbm, rout_ref), (cout_hbm, cout_ref),
+        ))
+    ]
+    for load in loads:
+        load.start()
+    loads[0].wait()
+    loads[1].wait()
+    mine = jnp.concatenate([x_ref[...].astype(F32), dy_ref[...].astype(F32)], axis=0).astype(BF16)
+    g1[z, y] = mine[:, 0:512]
+    g2[z, y] = mine[:, 512:1024]
+    vec_ref[...] = jnp.zeros_like(vec_ref)
     pl.semaphore_wait(barrier, len(greet))
 
     def y_copy(d):
-        return remote(ga.at[z, y], ga.at[z, y], yg_s.at[d], yg_r.at[d], at_y(d))
+        return remote(g1.at[z, y], g1.at[z, y], yg_s.at[d], yg_r.at[d], at_y(d))
 
     def z_copy(way, s, k):
         row = lax.rem(z + (NZ - s if way == 0 else s), NZ)
         col = lax.rem(y + NY - k, NY)
         return remote(
-            ga.at[row, col], ga.at[row, col], zg_s.at[way, s, k], zg_r.at[way, s, k],
+            g1.at[row, col], g1.at[row, col], zg_s.at[way, s, k], zg_r.at[way, s, k],
             at_z(1 if way == 0 else NZ - 1),
         )
+
+    def z2_copy(way, s):
+        row = lax.rem(z + (NZ - s if way == 0 else s), NZ)
+        ref = g2.at[row, y]
+        return remote(ref, ref, z2_s.at[way, s], z2_r.at[way, s], at_z(1 if way == 0 else NZ - 1))
+
+    def y2_copy(way, s, d):
+        row = lax.rem(z + (NZ - s if way == 0 else s), NZ)
+        ref = g2.at[row, y]
+        return remote(ref, ref, y2_s.at[way, s, d], y2_r.at[way, s, d], at_y(d))
 
     def pair(s):
         first = lax.rem(z + NZ - s, NZ)
@@ -132,13 +152,12 @@
         to = lax.rem(x + d, NX)
         return remote(sx.at[i, to], xr.at[i, x], xr_s.at[i, d], xr_r.at[i, d], at_x(d))
 
-    def xg_copy(s, d):
+    def xg_copy(s, k):
+        d, flip = k // 2, k % 2
         ref = hh.at[pair(s)[0], x]
-        return remote(ref, ref, xg_s.at[s - 1, d], xg_r.at[s - 1, d], at_x(d))
-
-    def cg_copy(s, d):
-        ref = hh.at[pair(s)[0], lax.rem(x + NX - d, NX)]
-        return remote(ref, ref, cg_s.at[s - 1, d], cg_r.at[s - 1, d], other)
+        core = 1 - c if flip else c
+        dev = (mp, lax.rem(x + d, NX) * 2 + core)
+        return remote(ref, ref, xg_s.at[s - 1, k], xg_r.at[s - 1, k], dev)
 
     def yi_copy(s, d):
         i = s - 1
@@ -151,7 +170,10 @@
 
     def project(s):
         cells = pair(s)
-        got = [split16(ga[cell], 1024) for cell in cells]
+        got = []
+        for cell in cells:
+            low, high = split16(g1[cell], 512), split16(g2[cell], 512)
+            got.append([jnp.concatenate([a, b], axis=1) for a, b in zip(low, high)])
         xb = jnp.concatenate([g[0] for g in got], axis=0)
         db = jnp.concatenate([g[1] for g in got], axis=0)
         pre = dot(xb, win_ref[...], ((1,), (0,)))
@@ -187,18 +209,12 @@
         hh[pair(s)[0], x] = jnp.concatenate(
             [pre * sig, up * (sig * (1.0 + pre * (1.0 - sig)))], axis=0
         ).astype(BF16)
-        for d in (2, 1, 3):
-            xg_copy(s, d).start()
-        cg_copy(s, 0).start()
-
-    def hand_over(s):
-        for d in (1, 3, 2):
-            xg_copy(s, d).wait_recv()
-            cg_copy(s, d).start()
+        for k in (4, 5, 2, 6, 3, 7, 1):
+            xg_copy(s, k).start()
 
     def back_project(s):
-        for d in (0, 1, 3, 2):
-            cg_copy(s, d).wait_recv()
+        for k in range(1, 8):
+            xg_copy(s, k).wait_recv()
         cells = pair(s)
         got = [split16(hh[cell], 512) for cell in cells]
         p = dot(jnp.concatenate([g[1] for g in got], axis=0), win_ref[...], ((1,), (1,)))
@@ -232,18 +248,38 @@
     for d in (2, 1, 3):
         y_copy(d).start()
     for way in range(2):
+        z2_copy(way, 0).start()
         z_copy(way, 0, 0).start()
+    for d in (2, 1, 3):
+        y2_copy(0, 0, d).start()
     for k in (1, 3, 2):
         y_copy(k).wait_recv()
         for way in range(2):
             z_copy(way, 0, k).start()
-    load_in.wait()
-    load_out.wait()
-
-    @pl.loop(1, 8 + LAG[3] + 1)
+    for way in range(2):
+        z2_copy(way, 0).wait_recv()
+        z2_copy(way, 1).start()
+        for d in (2, 1, 3):
+            y2_copy(way, 1, d).start()
+    for load in loads[2:]:
+        load.wait()
+
+    @pl.loop(1, 8 + LAG[2] + 1)
     def _(s):
         @pl.when(s < 7)
         def _():
+            for way in range(2):
+                z2_copy(way, s).wait_recv()
+                if way == 0:
+                    z2_copy(0, s + 1).start()
+                else:
+
+                    @pl.when(s < 6)
+                    def _():
+                        z2_copy(1, s + 1).start()
+
+                for d in (2, 1, 3):
+                    y2_copy(way, s + 1, d).start()
             for k in (0, 1, 3, 2):
                 for way in range(2):
                     z_copy(way, s - 1, k).wait_recv()
@@ -251,31 +287,43 @@
 
         @pl.when(s == 7)
         def _():
+            z2_copy(0, 7).wait_recv()
+            for d in (2, 1, 3):
+                y2_copy(0, 8, d).start()
             for k in (0, 1, 3, 2):
                 for way in range(2):
                     z_copy(way, 6, k).wait_recv()
                     if (k < 2) == (way == 0):
                         z_copy(way, 7, k).start()
 
+        @pl.when(s < 8)
+        def _():
+            for way in range(2):
+                for d in (1, 3, 2):
+                    y2_copy(way, s, d).wait_recv()
+
         @pl.when(s == 8)
         def _():
             for k in (0, 1, 3, 2):
                 z_copy(0 if k < 2 else 1, 7, k).wait_recv()
+            for d in (1, 3, 2):
+                y2_copy(0, 0, d).wait_recv()
+                y2_copy(0, 8, d).wait_recv()
 
         def stage(lag, run):
             @pl.when(jnp.logical_and(s > lag, s <= 8 + lag))
             def _():
                 run(s - lag)
 
-        stage(LAG[4], deliver)
-        stage(LAG[3], back_project)
-        stage(LAG[2], hand_over)
+        stage(LAG[0], spread)
         stage(LAG[1], activate)
-        stage(LAG[0], spread)
 
         @pl.when(s <= 8)
         def _():
             project(s)
+
+        stage(LAG[2], back_project)
+        stage(LAG[3], deliver)
 
     rp_out[...] = jnp.zeros_like(rp_out)
     cs_in[...] = jnp.zeros_like(cs_in)
@@ -296,6 +344,8 @@
 
     save_in = pltpu.make_async_copy(gin_ref, gin_hbm, o_sem.at[0])
     save_out = pltpu.make_async_copy(gout_ref, gout_hbm, o_sem.at[1])
+    save_ig = pltpu.make_async_copy(ig_ref, ig_hbm, o_sem.at[2])
+    save_vec = pltpu.make_async_copy(vec_ref, vec_hbm, o_sem.at[3])
     ones = jnp.ones((8, 128), F32)
 
     def my_copy(d):
@@ -324,10 +374,8 @@
     my[y] = jnp.concatenate([fold_lanes(row_sums_in, 8), fold_lanes(cs_out[...], 8)], axis=0)
     for d in range(1, NY):
         my_copy(d).start()
-    save_in.start()
-    save_out.start()
-
-    for s in range(8 + LAG[3] - LAG[4] + 1, 9):
+
+    for s in range(8 + LAG[2] - LAG[3] + 1, 9):
         deliver(s)
     zr[z] = zs[z]
 
@@ -336,11 +384,13 @@
     n_sum = nb[0]
     for k in range(1, 8):
         n_sum = n_sum + nb[k]
-    cin_new[...] = DECAY * cin_ref[...] + (1.0 - DECAY) * (unfold_lanes(n_sum, 0, 4) / D + EPS)
-    rout_new[...] = DECAY * rout_ref[...] + (1.0 - DECAY) * (unfold_lanes(n_sum, 4, 4) / D + EPS)
-
-    inv_cin = 1.0 / cin_new[...]
-    rp_out[...] = columns_of(1.0 / rout_new[...])
+    cin_new = DECAY * cin_ref[...] + (1.0 - DECAY) * (unfold_lanes(n_sum, 0, 4) / D + EPS)
+    rout_new = DECAY * rout_ref[...] + (1.0 - DECAY) * (unfold_lanes(n_sum, 4, 4) / D + EPS)
+    vec_ref[2:3, 0:512] = cin_new
+    vec_ref[2:3, 512:1024] = rout_new
+
+    inv_cin = 1.0 / cin_new
+    rp_out[...] = columns_of(1.0 / rout_new)
 
     @pl.loop(0, 4)
     def _(j):
@@ -360,18 +410,16 @@
 
     for d in range(1, NY):
         my_copy(d).wait_recv()
-    mz[z] = (my[0] + my[1]) + (my[2] + my[3])
-
-    @pl.loop(1, NZ)
-    def _(d):
+    mz[z] = ((my[0] + my[1]) + (my[2] + my[3])).astype(BF16)
+
+    for d in FAR_FIRST:
         mz_copy(d).start()
 
     for d in range(1, NY):
         ty_copy(d).wait_recv()
     tz[z] = ((ty[0] + ty[1]) + (ty[2] + ty[3])).astype(BF16)
 
-    @pl.loop(1, NZ)
-    def _(d):
+    for d in FAR_FIRST:
         tz_copy(d).start()
 
     @pl.loop(1, NZ)
@@ -382,19 +430,39 @@
     for k in range(1, NZ):
         t = t + zr[k].astype(F32)
     ig_ref[...] = jnp.concatenate([t[0:8], t[8:16]], axis=1).astype(BF16)
+    save_ig.start()
 
     @pl.loop(1, NZ)
     def _(d):
         mz_copy(d).wait_recv()
 
-    m_sum = mz[0]
+    m_sum = mz[0].astype(F32)
     for k in range(1, NZ):
-        m_sum = m_sum + mz[k]
+        m_sum = m_sum + mz[k].astype(F32)
     r_new = DECAY * rin_ref[...] + (1.0 - DECAY) * (unfold_lanes(m_sum, 0, 8) / FF + EPS)
     c_new = DECAY * cout_ref[...] + (1.0 - DECAY) * (unfold_lanes(m_sum, 8, 8) / FF + EPS)
-    rin_new[...] = r_new
-    cout_new[...] = c_new
+    vec_ref[0:1, :] = r_new
+    vec_ref[1:2, :] = c_new
     inv_r, inv_c = fold_lanes(1.0 / r_new, 8), fold_lanes(1.0 / c_new, 8)
+
+    rp_in[...] = columns_of(r_new)
+    rp_out[...] = columns_of(rout_new)
+
+    @pl.loop(0, 8)
+    def _(j):
+        rows = pl.ds(pl.multiple_of(j * 128, 128), 128)
+        r = rp_in[rows, :]
+        for k in range(4):
+            lanes = slice(k * 128, (k + 1) * 128)
+            gin_ref[rows, lanes] = gin_ref[rows, lanes] * lax.rsqrt(r * vec_ref[2:3, lanes])
+        rows = pl.ds(pl.multiple_of(j * 64, 64), 64)
+        r = rp_out[rows, :]
+        for k in range(8):
+            lanes = slice(k * 128, (k + 1) * 128)
+            gout_ref[rows, lanes] = gout_ref[rows, lanes] * lax.rsqrt(r * vec_ref[1:2, lanes])
+
+    save_in.start()
+    save_out.start()
 
     @pl.loop(1, NZ)
     def _(d):
@@ -415,12 +483,11 @@
     for k in range(1, 8):
         t = t + nn[k]
     total = jnp.sum(t, axis=1, keepdims=True)
-    den_ref[...] = jnp.broadcast_to(
-        jnp.maximum(CLIP, jnp.sqrt(total / (float(D) * float(FF)))), (8, 128)
-    )
-
-    save_in.wait()
-    save_out.wait()
+    inv = 1.0 / jnp.maximum(CLIP, jnp.sqrt(total / (float(D) * float(FF))))
+    vec_ref[3:4, 0:512] = jnp.broadcast_to(inv[0:1], (1, 512))
+    vec_ref[3:4, 512:1024] = jnp.broadcast_to(inv[4:5], (1, 512))
+    save_vec.start()
+
     for d in range(1, NY):
         y_copy(d).wait_send()
         my_copy(d).wait_send()
@@ -429,11 +496,10 @@
     @pl.loop(1, 9)
     def _(s):
         cx_copy(s).wait_send()
-        cg_copy(s, 0).wait_send()
+        for k in range(1, 8):
+            xg_copy(s, k).wait_send()
         for d in range(1, NX):
             xr_copy(s, d).wait_send()
-            xg_copy(s, d).wait_send()
-            cg_copy(s, d).wait_send()
             yi_copy(s, d).wait_send()
 
     for d in range(1, 8):
@@ -445,9 +511,17 @@
         for k in range(NY):
             for way in range(2):
                 z_copy(way, s, k).wait_send()
+        for way in range(2):
+            z2_copy(way, s).wait_send()
+            for d in range(1, NY):
+                y2_copy(way, s + 1, d).wait_send()
 
     for k in range(NY):
         z_copy(0 if k < 2 else 1, 7, k).wait_send()
+    z2_copy(0, 7).wait_send()
+    for d in range(1, NY):
+        y2_copy(0, 0, d).wait_send()
+        y2_copy(0, 8, d).wait_send()
 
     @pl.loop(1, NZ)
     def _(d):
@@ -455,8 +529,10 @@
         tz_copy(d).wait_send()
         zi_copy(d).wait_send()
 
-
-VMEM_SPEC = pl.BlockSpec(memory_space=pltpu.VMEM)
+    for save in (save_in, save_out, save_ig, save_vec):
+        save.wait()
+
+
 ANY_SPEC = pl.BlockSpec(memory_space=pl.ANY)
 
 
@@ -466,13 +542,14 @@
     shape = jax.ShapeDtypeStruct
     outs = (
         shape((8, 1024), BF16), shape((1024, 512), F32), shape((512, 1024), F32),
-        shape((1, 1024), F32), shape((1, 512), F32), shape((1, 512), F32), shape((1, 1024), F32),
-        shape((8, 128), F32),
+        shape((8, 1024), F32),
     )
     scratch = [
-        vmem((1024, 512), BF16), vmem((512, 1024), BF16),
-        vmem((1024, 512), F32), vmem((512, 1024), F32),
-        vmem((NZ, NY, 16, 1024), BF16), vmem((512, 1024), BF16), vmem((512, 1024), BF16),
+        vmem((8, 1024), BF16), vmem((8, 1024), BF16), vmem((1024, 512), BF16), vmem((512, 1024), BF16),
+        vmem((1, 1024), F32), vmem((1, 512), F32), vmem((1, 512), F32), vmem((1, 1024), F32),
+        vmem((8, 1024), BF16), vmem((1024, 512), F32), vmem((512, 1024), F32), vmem((8, 1024), F32),
+        vmem((NZ, NY, 16, 512), BF16), vmem((NZ, NY, 16, 512), BF16),
+        vmem((512, 1024), BF16), vmem((512, 1024), BF16),
         vmem((512, 512), BF16), vmem((512, 512), BF16),
         vmem((8, 2, 32, 512), F32), vmem((8, 2, 32, 512), F32), vmem((8, 2, 32, 512), F32),
         vmem((8, NX, 16, 512), F32), vmem((8, NX, 16, 512), BF16), vmem((8, NX, 16, 512), BF16),
@@ -480,12 +557,13 @@
         vmem((8, NY, 2, 16, 512), BF16), vmem((8, NY, 2, 16, 512), BF16),
         vmem((NZ, 16, 512), BF16), vmem((NZ, 16, 512), BF16),
         vmem((1024, 128), F32), vmem((512, 128), F32), vmem((1, 512), F32), vmem((1, 1024), F32),
-        vmem((NY, 16, 128), F32), vmem((NZ, 16, 128), F32),
+        vmem((NY, 16, 128), F32), vmem((NZ, 16, 128), BF16),
         vmem((NY, 16, 128), F32), vmem((NZ, 16, 128), BF16),
         vmem((8, 8, 128), F32), vmem((8, 8, 128), F32),
-        dma((2,)), dma((2,)),
-        dma((NY,)), dma((NY,)), dma((2, 8, NY)), dma((2, 8, NY)), dma((8,)), dma((8,)),
-        dma((8, NX)), dma((8, NX)), dma((8, NX)), dma((8, NX)), dma((8, NX)), dma((8, NX)),
+        dma((8,)), dma((4,)),
+        dma((NY,)), dma((NY,)), dma((2, 8, NY)), dma((2, 8, NY)),
+        dma((2, 9, NY)), dma((2, 9, NY)), dma((2, 8)), dma((2, 8)), dma((8,)), dma((8,)),
+        dma((8, NX)), dma((8, NX)), dma((8, 8)), dma((8, 8)),
         dma((8, NY)), dma((8, NY)), dma((NZ,)), dma((NZ,)),
         dma((NY,)), dma((NY,)), dma((NZ,)), dma((NZ,)),
         dma((NY,)), dma((NY,)), dma((NZ,)), dma((NZ,)),
@@ -494,8 +572,8 @@
     return pl.pallas_call(
         kernel,
         out_shape=outs,
-        in_specs=[VMEM_SPEC, VMEM_SPEC, ANY_SPEC, ANY_SPEC] + [VMEM_SPEC] * 4,
-        out_specs=[VMEM_SPEC, ANY_SPEC, ANY_SPEC] + [VMEM_SPEC] * 5,
+        in_specs=[ANY_SPEC] * 8,
+        out_specs=[ANY_SPEC] * 4,
         scratch_shapes=scratch,
         compiler_params=pltpu.CompilerParams(
             collective_id=1, has_side_effects=True, vmem_limit_bytes=56 * 2**20
@@ -510,36 +588,23 @@
 
 
 def scale_kernel(
-    ig_ref, gin_ref, gout_ref, rin_ref, cin_ref, rout_ref, cout_ref, den_ref,
+    ig_ref, gin_ref, gout_ref, vec_ref,
     ig_out, uin_ref, uout_ref, rin_out, cin_out, rout_out, cout_out,
 ):
-    j = pl.program_id(0)
-
-    @pl.when(j == 0)
+    @pl.when(pl.program_id(0) == 0)
     def _():
         ig_out[...] = ig_ref[...]
-        rin_out[...] = fold_lanes(rin_ref[...], 8)
-        cin_out[...] = fold_lanes(cin_ref[...], 4)
-        rout_out[...] = fold_lanes(rout_ref[...], 4)
-        cout_out[...] = fold_lanes(cout_ref[...], 8)
-
-    def update(g_ref, row, col_ref, den, u_ref):
-        r = columns_of(row)
-        for k in range(g_ref.shape[1] // 128):
-            lanes = slice(k * 128, (k + 1) * 128)
-            u_ref[:, lanes] = (
-                g_ref[:, lanes] * lax.rsqrt(r * col_ref[:, lanes]) / den
-            ).astype(BF16)
-
-    many, few = 1024 // STEPS, 512 // STEPS
-    update(
-        gin_ref, rin_ref[:, pl.ds(pl.multiple_of(j * many, many), many)], cin_ref,
-        den_ref[0:1, :], uin_ref,
-    )
-    update(
-        gout_ref, rout_ref[:, pl.ds(pl.multiple_of(j * few, few), few)], cout_ref,
-        den_ref[4:5, :], uout_ref,
-    )
+        rin_out[...] = fold_lanes(vec_ref[0:1, :], 8)
+        cout_out[...] = fold_lanes(vec_ref[1:2, :], 8)
+        cin_out[...] = fold_lanes(vec_ref[2:3, 0:512], 4)
+        rout_out[...] = fold_lanes(vec_ref[2:3, 512:1024], 4)
+
+    inv_in = vec_ref[3:4, 0:512]
+    inv_out = vec_ref[3:4, 512:1024]
+    uin_ref[...] = (gin_ref[...] * inv_in).astype(BF16)
+    for k in range(2):
+        lanes = slice(k * 512, (k + 1) * 512)
+        uout_ref[:, lanes] = (gout_ref[:, lanes] * inv_out).astype(BF16)
 
 
 def scale(*args):
@@ -550,8 +615,7 @@
         scale_kernel,
         grid=(STEPS,),
         in_specs=[
-            whole(8, 1024), big(1024 // STEPS, 512), big(512 // STEPS, 1024),
-            whole(1, 1024), whole(1, 512), whole(1, 512), whole(1, 1024), whole(8, 128),
+            whole(8, 1024), big(1024 // STEPS, 512), big(512 // STEPS, 1024), whole(8, 1024),
         ],
         out_specs=[
             whole(8, 1024), big(1024 // STEPS, 512), big(512 // STEPS, 1024),

time: 96.3 us -> 90.1 us (0.936)
  Pallas kernels: 95.4 us -> 89.2 us
    pallas_call x1, Pallas kernels: 90.8 us -> 85 us  [step(): pl.pallas_call(kernel, out_shape=outs, in_specs=[ANY_SPEC] * 8, out_specs...]
where the time goes in v3:
time: 90.1 us; the launch traced here: 89.8 us
  Pallas kernels  89.2 us (99%)
    pallas_call x1, Pallas kernels, step(): pl.pallas_call(kernel, out_shape=outs, in_specs=[ANY_SPEC] * 8, out_specs...  85 us
    pallas_call x1, Pallas kernels, scale(): pl.pallas_call(scale_kernel, grid=(STEPS,), in_specs=[whole(8, 1024), big...  4.19 us

profile of v3, /device:TPU:1, one launch (start us, length us, event | category | flops | bytes accessed | tf_op | source)
XLA Modules:
  0.0 89.8 jit_solution(16484657394613173428)
XLA Ops:
  0.6 85.0 %shard_map.135 = (bf16[8,1024]{1,0:T(8,128)(2,1)}, f32[1024,512]{1,0:T(8,128)}, f32[512,1024]{1,0:T(8,128)}, f32[8,1024]{1,0:T(8,128)}) custom-call(bf16[8,1024]{1,0:T(8,128)(2,1)} %x_hbm.1, bf16[8,1024]{1,0:T(8,128)(2,1)} %dy_hbm.1, bf16[1024,512]{1,0:T(8,128)(2,1)} %win_hbm.1, bf16[512,1024]{1,0:T(8,128)(2,1)} %wout_hbm.1, f32[1,1024]{1,0:T(1,128)} %bitcast.8, ...), custom_call_target="tpu_custom_call" | custom-call | flops 2700000000 | bytes 8388608 | tf_op jit(solution)/shard_map/pallas_call | solution.py:572
  85.7 4.2 %shard_map.136 = (bf16[8,1024]{1,0:T(8,128)(2,1)}, bf16[1024,512]{1,0:T(8,128)(2,1)}, bf16[512,1024]{1,0:T(8,128)(2,1)}, f32[8,128]{1,0:T(8,128)}, f32[4,128]{1,...) custom-call(bf16[8,1024]{1,0:T(8,128)(2,1)} %get-tuple-element.18.ig_ref, f32[1024,512]{1,0:T(8,128)} %get-tuple-element.19.gin_ref, ...), custom_call_target="tpu_custom_call" | custom-call | tf_op jit(solution)/shard_map/pallas_call | solution.py:614

commit v4 on v3

--- a/solution.py
+++ b/solution.py
@@ -18,6 +18,7 @@
 MESH = pl.DeviceIdType.MESH
 EXACT = lax.Precision.HIGHEST
 LAG = (1, 3, 5, 7)
+FIRST = 256
 FAR_FIRST = (8, 7, 9, 6, 10, 5, 11, 4, 12, 3, 13, 2, 14, 1, 15)
 
 
@@ -86,7 +87,7 @@
         )
 
     barrier = pltpu.get_barrier_semaphore()
-    greet = [at_y(1), at_y(2), at_y(3), at_z(1), at_z(NZ - 1), at_x(1), at_x(2), at_x(3), other]
+    greet = [at_y(1), at_y(2), at_y(3), at_z(1), at_z(NZ - 1), at_z(2), at_z(NZ - 2), at_x(1), at_x(2), at_x(3), other]
     for dev in greet:
         pl.semaphore_signal(barrier, inc=1, device_id=dev, device_id_type=MESH)
 
@@ -102,26 +103,29 @@
     loads[0].wait()
     loads[1].wait()
     mine = jnp.concatenate([x_ref[...].astype(F32), dy_ref[...].astype(F32)], axis=0).astype(BF16)
-    g1[z, y] = mine[:, 0:512]
-    g2[z, y] = mine[:, 512:1024]
+    g1[z, y] = mine[:, 0:FIRST]
+    g2[z, y] = mine[:, FIRST:1024]
     vec_ref[...] = jnp.zeros_like(vec_ref)
     pl.semaphore_wait(barrier, len(greet))
 
     def y_copy(d):
         return remote(g1.at[z, y], g1.at[z, y], yg_s.at[d], yg_r.at[d], at_y(d))
 
-    def z_copy(way, s, k):
-        row = lax.rem(z + (NZ - s if way == 0 else s), NZ)
-        col = lax.rem(y + NY - k, NY)
-        return remote(
-            g1.at[row, col], g1.at[row, col], zg_s.at[way, s, k], zg_r.at[way, s, k],
-            at_z(1 if way == 0 else NZ - 1),
-        )
-
-    def z2_copy(way, s):
-        row = lax.rem(z + (NZ - s if way == 0 else s), NZ)
+    def z_way(way, r):
+        hop = jnp.where(r > 1, 2, 1)
+        back = r - hop
+        row = lax.rem(z + (NZ - back if way == 0 else back), NZ)
+        return row, at_z(hop if way == 0 else NZ - hop)
+
+    def z_copy(way, r, k):
+        row, dev = z_way(way, r)
+        ref = g1.at[row, lax.rem(y + NY - k, NY)]
+        return remote(ref, ref, zg_s.at[way, r, k], zg_r.at[way, r, k], dev)
+
+    def z2_copy(way, r):
+        row, dev = z_way(way, r)
         ref = g2.at[row, y]
-        return remote(ref, ref, z2_s.at[way, s], z2_r.at[way, s], at_z(1 if way == 0 else NZ - 1))
+        return remote(ref, ref, z2_s.at[way, r], z2_r.at[way, r], dev)
 
     def y2_copy(way, s, d):
         row = lax.rem(z + (NZ - s if way == 0 else s), NZ)
@@ -172,7 +176,7 @@
         cells = pair(s)
         got = []
         for cell in cells:
-            low, high = split16(g1[cell], 512), split16(g2[cell], 512)
+            low, high = split16(g1[cell], FIRST), split16(g2[cell], 1024 - FIRST)
             got.append([jnp.concatenate([a, b], axis=1) for a, b in zip(low, high)])
         xb = jnp.concatenate([g[0] for g in got], axis=0)
         db = jnp.concatenate([g[1] for g in got], axis=0)
@@ -247,54 +251,66 @@
 
     for d in (2, 1, 3):
         y_copy(d).start()
-    for way in range(2):
-        z2_copy(way, 0).start()
-        z_copy(way, 0, 0).start()
+    for r in (2, 1):
+        for way in range(2):
+            z2_copy(way, r).start()
+            z_copy(way, r, 0).start()
+    for k in (1, 3, 2):
+        y_copy(k).wait_recv()
+        for r in (2, 1):
+            for way in range(2):
+                z_copy(way, r, k).start()
+    for r in (1, 2):
+        for way in range(2):
+            z2_copy(way, r).wait_recv()
+            z2_copy(way, r + 2).start()
+            for d in (2, 1, 3):
+                y2_copy(way, r, d).start()
     for d in (2, 1, 3):
         y2_copy(0, 0, d).start()
-    for k in (1, 3, 2):
-        y_copy(k).wait_recv()
-        for way in range(2):
-            z_copy(way, 0, k).start()
-    for way in range(2):
-        z2_copy(way, 0).wait_recv()
-        z2_copy(way, 1).start()
-        for d in (2, 1, 3):
-            y2_copy(way, 1, d).start()
     for load in loads[2:]:
         load.wait()
 
     @pl.loop(1, 8 + LAG[2] + 1)
     def _(s):
-        @pl.when(s < 7)
+        @pl.when(s < 6)
         def _():
-            for way in range(2):
-                z2_copy(way, s).wait_recv()
-                if way == 0:
-                    z2_copy(0, s + 1).start()
-                else:
-
-                    @pl.when(s < 6)
-                    def _():
-                        z2_copy(1, s + 1).start()
-
-                for d in (2, 1, 3):
-                    y2_copy(way, s + 1, d).start()
             for k in (0, 1, 3, 2):
                 for way in range(2):
-                    z_copy(way, s - 1, k).wait_recv()
-                    z_copy(way, s, k).start()
-
-        @pl.when(s == 7)
+                    z_copy(way, s, k).wait_recv()
+                    z_copy(way, s + 2, k).start()
+            for way in range(2):
+                z2_copy(way, s + 2).wait_recv()
+                if way == 0:
+
+                    @pl.when(s < 5)
+                    def _():
+                        z2_copy(0, s + 4).start()
+                else:
+
+                    @pl.when(s < 4)
+                    def _():
+                        z2_copy(1, s + 4).start()
+
+                for d in (2, 1, 3):
+                    y2_copy(way, s + 2, d).start()
+
+        @pl.when(s == 6)
         def _():
-            z2_copy(0, 7).wait_recv()
-            for d in (2, 1, 3):
-                y2_copy(0, 8, d).start()
             for k in (0, 1, 3, 2):
                 for way in range(2):
                     z_copy(way, 6, k).wait_recv()
                     if (k < 2) == (way == 0):
-                        z_copy(way, 7, k).start()
+                        z_copy(way, 8, k).start()
+            z2_copy(0, 8).wait_recv()
+            for d in (2, 1, 3):
+                y2_copy(0, 8, d).start()
+
+        @pl.when(s == 7)
+        def _():
+            for k in (0, 1, 3, 2):
+                for way in range(2):
+                    z_copy(way, 7, k).wait_recv()
 
         @pl.when(s < 8)
         def _():
@@ -305,7 +321,7 @@
         @pl.when(s == 8)
         def _():
             for k in (0, 1, 3, 2):
-                z_copy(0 if k < 2 else 1, 7, k).wait_recv()
+                z_copy(0 if k < 2 else 1, 8, k).wait_recv()
             for d in (1, 3, 2):
                 y2_copy(0, 0, d).wait_recv()
                 y2_copy(0, 8, d).wait_recv()
@@ -506,19 +522,18 @@
         nb_copy(d).wait_send()
         nn_copy(d).wait_send()
 
-    @pl.loop(0, 7)
+    @pl.loop(1, 8)
     def _(s):
-        for k in range(NY):
-            for way in range(2):
-                z_copy(way, s, k).wait_send()
         for way in range(2):
             z2_copy(way, s).wait_send()
+            for k in range(NY):
+                z_copy(way, s, k).wait_send()
             for d in range(1, NY):
-                y2_copy(way, s + 1, d).wait_send()
+                y2_copy(way, s, d).wait_send()
 
     for k in range(NY):
-        z_copy(0 if k < 2 else 1, 7, k).wait_send()
-    z2_copy(0, 7).wait_send()
+        z_copy(0 if k < 2 else 1, 8, k).wait_send()
+    z2_copy(0, 8).wait_send()
     for d in range(1, NY):
         y2_copy(0, 0, d).wait_send()
         y2_copy(0, 8, d).wait_send()
@@ -548,7 +563,7 @@
         vmem((8, 1024), BF16), vmem((8, 1024), BF16), vmem((1024, 512), BF16), vmem((512, 1024), BF16),
         vmem((1, 1024), F32), vmem((1, 512), F32), vmem((1, 512), F32), vmem((1, 1024), F32),
         vmem((8, 1024), BF16), vmem((1024, 512), F32), vmem((512, 1024), F32), vmem((8, 1024), F32),
-        vmem((NZ, NY, 16, 512), BF16), vmem((NZ, NY, 16, 512), BF16),
+        vmem((NZ, NY, 16, FIRST), BF16), vmem((NZ, NY, 16, 1024 - FIRST), BF16),
         vmem((512, 1024), BF16), vmem((512, 1024), BF16),
         vmem((512, 512), BF16), vmem((512, 512), BF16),
         vmem((8, 2, 32, 512), F32), vmem((8, 2, 32, 512), F32), vmem((8, 2, 32, 512), F32),
@@ -561,8 +576,8 @@
         vmem((NY, 16, 128), F32), vmem((NZ, 16, 128), BF16),
         vmem((8, 8, 128), F32), vmem((8, 8, 128), F32),
         dma((8,)), dma((4,)),
-        dma((NY,)), dma((NY,)), dma((2, 8, NY)), dma((2, 8, NY)),
-        dma((2, 9, NY)), dma((2, 9, NY)), dma((2, 8)), dma((2, 8)), dma((8,)), dma((8,)),
+        dma((NY,)), dma((NY,)), dma((2, 9, NY)), dma((2, 9, NY)),
+        dma((2, 9, NY)), dma((2, 9, NY)), dma((2, 9)), dma((2, 9)), dma((8,)), dma((8,)),
         dma((8, NX)), dma((8, NX)), dma((8, 8)), dma((8, 8)),
         dma((8, NY)), dma((8, NY)), dma((NZ,)), dma((NZ,)),
         dma((NY,)), dma((NY,)), dma((NZ,)), dma((NZ,)),
@@ -584,7 +599,7 @@
     )(*args)
 
 
-STEPS = 4
+STEPS = 2
 
 
 def scale_kernel(

time: 90.1 us -> 83.9 us (0.931)
  Pallas kernels: 89.2 us -> 83.1 us
    pallas_call x1, Pallas kernels: 85 us -> 79.8 us  [step(): pl.pallas_call(kernel, out_shape=outs, in_specs=[ANY_SPEC] * 8, out_specs...]
where the time goes in v4:
time: 83.9 us; the launch traced here: 83.7 us
  Pallas kernels  83.1 us (99%)
    pallas_call x1, Pallas kernels, step(): pl.pallas_call(kernel, out_shape=outs, in_specs=[ANY_SPEC] * 8, out_specs...  79.8 us
    pallas_call x1, Pallas kernels, scale(): pl.pallas_call(scale_kernel, grid=(STEPS,), in_specs=[whole(8, 1024), big...  3.31 us

profile of v4, /device:TPU:1, one launch (start us, length us, event | category | flops | bytes accessed | tf_op | source)
XLA Modules:
  0.0 83.7 jit_solution(398818622494610770)
XLA Ops:
  0.6 79.8 %shard_map.135 = (bf16[8,1024]{1,0:T(8,128)(2,1)}, f32[1024,512]{1,0:T(8,128)}, f32[512,1024]{1,0:T(8,128)}, f32[8,1024]{1,0:T(8,128)}) custom-call(bf16[8,1024]{1,0:T(8,128)(2,1)} %x_hbm.1, bf16[8,1024]{1,0:T(8,128)(2,1)} %dy_hbm.1, bf16[1024,512]{1,0:T(8,128)(2,1)} %win_hbm.1, bf16[512,1024]{1,0:T(8,128)(2,1)} %wout_hbm.1, f32[1,1024]{1,0:T(1,128)} %bitcast.8, ...), custom_call_target="tpu_custom_call" | custom-call | flops 2700000000 | bytes 8388608 | tf_op jit(solution)/shard_map/pallas_call | solution.py:587
  80.4 3.3 %shard_map.136 = (bf16[8,1024]{1,0:T(8,128)(2,1)}, bf16[1024,512]{1,0:T(8,128)(2,1)}, bf16[512,1024]{1,0:T(8,128)(2,1)}, f32[8,128]{1,0:T(8,128)}, f32[4,128]{1,...) custom-call(bf16[8,1024]{1,0:T(8,128)(2,1)} %get-tuple-element.18.ig_ref, f32[1024,512]{1,0:T(8,128)} %get-tuple-element.19.gin_ref, ...), custom_call_target="tpu_custom_call" | custom-call | tf_op jit(solution)/shard_map/pallas_call | solution.py:629

commit v5 on v4

--- a/solution.py
+++ b/solution.py
@@ -438,6 +438,39 @@
     for d in FAR_FIRST:
         tz_copy(d).start()
 
+    for d in range(1, NY):
+        y_copy(d).wait_send()
+        my_copy(d).wait_send()
+        ty_copy(d).wait_send()
+
+    @pl.loop(1, 9)
+    def _(s):
+        cx_copy(s).wait_send()
+        for k in range(1, 8):
+            xg_copy(s, k).wait_send()
+        for d in range(1, NX):
+            xr_copy(s, d).wait_send()
+            yi_copy(s, d).wait_send()
+
+    for d in range(1, 8):
+        nb_copy(d).wait_send()
+
+    @pl.loop(1, 8)
+    def _(s):
+        for way in range(2):
+            z2_copy(way, s).wait_send()
+            for k in range(NY):
+                z_copy(way, s, k).wait_send()
+            for d in range(1, NY):
+                y2_copy(way, s, d).wait_send()
+
+    for k in range(NY):
+        z_copy(0 if k < 2 else 1, 8, k).wait_send()
+    z2_copy(0, 8).wait_send()
+    for d in range(1, NY):
+        y2_copy(0, 0, d).wait_send()
+        y2_copy(0, 8, d).wait_send()
+
     @pl.loop(1, NZ)
     def _(d):
         zi_copy(d).wait_recv()
@@ -493,6 +526,12 @@
     nn[nar] = jnp.where(which < 4, n_in, n_out)
     for d in range(1, 8):
         nn_copy(d).start()
+    @pl.loop(1, NZ)
+    def _(d):
+        mz_copy(d).wait_send()
+        tz_copy(d).wait_send()
+        zi_copy(d).wait_send()
+
     for d in range(1, 8):
         nn_copy(d).wait_recv()
     t = nn[0]
@@ -504,46 +543,8 @@
     vec_ref[3:4, 512:1024] = jnp.broadcast_to(inv[4:5], (1, 512))
     save_vec.start()
 
-    for d in range(1, NY):
-        y_copy(d).wait_send()
-        my_copy(d).wait_send()
-        ty_copy(d).wait_send()
-
-    @pl.loop(1, 9)
-    def _(s):
-        cx_copy(s).wait_send()
-        for k in range(1, 8):
-            xg_copy(s, k).wait_send()
-        for d in range(1, NX):
-            xr_copy(s, d).wait_send()
-            yi_copy(s, d).wait_send()
-
     for d in range(1, 8):
-        nb_copy(d).wait_send()
         nn_copy(d).wait_send()
-
-    @pl.loop(1, 8)
-    def _(s):
-        for way in range(2):
-            z2_copy(way, s).wait_send()
-            for k in range(NY):
-                z_copy(way, s, k).wait_send()
-            for d in range(1, NY):
-                y2_copy(way, s, d).wait_send()
-
-    for k in range(NY):
-        z_copy(0 if k < 2 else 1, 8, k).wait_send()
-    z2_copy(0, 8).wait_send()
-    for d in range(1, NY):
-        y2_copy(0, 0, d).wait_send()
-        y2_copy(0, 8, d).wait_send()
-
-    @pl.loop(1, NZ)
-    def _(d):
-        mz_copy(d).wait_send()
-        tz_copy(d).wait_send()
-        zi_copy(d).wait_send()
-
     for save in (save_in, save_out, save_ig, save_vec):
         save.wait()
 

time: 83.9 us -> 83.9 us (level)
  no operation moved by 1% of the time
where the time goes in v5:
time: 83.9 us; the launch traced here: 83.7 us
  Pallas kernels  83.1 us (99%)
    pallas_call x1, Pallas kernels, step(): pl.pallas_call(kernel, out_shape=outs, in_specs=[ANY_SPEC] * 8, out_specs...  79.8 us
    pallas_call x1, Pallas kernels, scale(): pl.pallas_call(scale_kernel, grid=(STEPS,), in_specs=[whole(8, 1024), big...  3.31 us

profile of v5, /device:TPU:1, one launch (start us, length us, event | category | flops | bytes accessed | tf_op | source)
XLA Modules:
  0.0 83.7 jit_solution(2673554934843360531)
XLA Ops:
  0.6 79.8 %shard_map.135 = (bf16[8,1024]{1,0:T(8,128)(2,1)}, f32[1024,512]{1,0:T(8,128)}, f32[512,1024]{1,0:T(8,128)}, f32[8,1024]{1,0:T(8,128)}) custom-call(bf16[8,1024]{1,0:T(8,128)(2,1)} %x_hbm.1, bf16[8,1024]{1,0:T(8,128)(2,1)} %dy_hbm.1, bf16[1024,512]{1,0:T(8,128)(2,1)} %win_hbm.1, bf16[512,1024]{1,0:T(8,128)(2,1)} %wout_hbm.1, f32[1,1024]{1,0:T(1,128)} %bitcast.8, ...), custom_call_target="tpu_custom_call" | custom-call | flops 2700000000 | bytes 8388608 | tf_op jit(solution)/shard_map/pallas_call | solution.py:588
  80.4 3.3 %shard_map.136 = (bf16[8,1024]{1,0:T(8,128)(2,1)}, bf16[1024,512]{1,0:T(8,128)(2,1)}, bf16[512,1024]{1,0:T(8,128)(2,1)}, f32[8,128]{1,0:T(8,128)}, f32[4,128]{1,...) custom-call(bf16[8,1024]{1,0:T(8,128)(2,1)} %get-tuple-element.18.ig_ref, f32[1024,512]{1,0:T(8,128)} %get-tuple-element.19.gin_ref, ...), custom_call_target="tpu_custom_call" | custom-call | tf_op jit(solution)/shard_map/pallas_call | solution.py:630

commit v6 on v5

--- a/solution.py
+++ b/solution.py
@@ -49,14 +49,13 @@
 
 def kernel(
     x_hbm, dy_hbm, win_hbm, wout_hbm, rin_hbm, cin_hbm, rout_hbm, cout_hbm,
-    ig_hbm, gin_hbm, gout_hbm, vec_hbm,
+    ig_ref, gin_ref, gout_ref, vec_ref,
     x_ref, dy_ref, win_ref, wout_ref, rin_ref, cin_ref, rout_ref, cout_ref,
-    ig_ref, gin_ref, gout_ref, vec_ref,
     g1, g2, xs, ds, acts, hgs, keep, give, cx, tot, sx, xr, hh,
     ys, yr, zs, zr,
     rp_in, rp_out, cs_in, cs_out,
     my, mz, ty, tz, nb, nn,
-    w_sem, o_sem,
+    w_sem,
     yg_s, yg_r, zg_s, zg_r, y2_s, y2_r, z2_s, z2_r, cx_s, cx_r, xr_s, xr_r, xg_s, xg_r,
     yi_s, yi_r, zi_s, zi_r, my_s, my_r, mz_s, mz_r, ty_s, ty_r, tz_s, tz_r,
     nb_s, nb_r, nn_s, nn_r,
@@ -358,10 +357,6 @@
         cs_in[...] += jnp.sum(q, axis=0, keepdims=True)
         rp_in[cols, :] = lane_fold(q)
 
-    save_in = pltpu.make_async_copy(gin_ref, gin_hbm, o_sem.at[0])
-    save_out = pltpu.make_async_copy(gout_ref, gout_hbm, o_sem.at[1])
-    save_ig = pltpu.make_async_copy(ig_ref, ig_hbm, o_sem.at[2])
-    save_vec = pltpu.make_async_copy(vec_ref, vec_hbm, o_sem.at[3])
     ones = jnp.ones((8, 128), F32)
 
     def my_copy(d):
@@ -479,7 +474,6 @@
     for k in range(1, NZ):
         t = t + zr[k].astype(F32)
     ig_ref[...] = jnp.concatenate([t[0:8], t[8:16]], axis=1).astype(BF16)
-    save_ig.start()
 
     @pl.loop(1, NZ)
     def _(d):
@@ -509,9 +503,6 @@
         for k in range(8):
             lanes = slice(k * 128, (k + 1) * 128)
             gout_ref[rows, lanes] = gout_ref[rows, lanes] * lax.rsqrt(r * vec_ref[1:2, lanes])
-
-    save_in.start()
-    save_out.start()
 
     @pl.loop(1, NZ)
     def _(d):
@@ -541,14 +532,12 @@
     inv = 1.0 / jnp.maximum(CLIP, jnp.sqrt(total / (float(D) * float(FF))))
     vec_ref[3:4, 0:512] = jnp.broadcast_to(inv[0:1], (1, 512))
     vec_ref[3:4, 512:1024] = jnp.broadcast_to(inv[4:5], (1, 512))
-    save_vec.start()
 
     for d in range(1, 8):
         nn_copy(d).wait_send()
-    for save in (save_in, save_out, save_ig, save_vec):
-        save.wait()
-
-
+
+
+VMEM_SPEC = pl.BlockSpec(memory_space=pltpu.VMEM)
 ANY_SPEC = pl.BlockSpec(memory_space=pl.ANY)
 
 
@@ -557,13 +546,12 @@
     vmem = pltpu.VMEM
     shape = jax.ShapeDtypeStruct
     outs = (
-        shape((8, 1024), BF16), shape((1024, 512), F32), shape((512, 1024), F32),
-        shape((8, 1024), F32),
+        vmem((8, 1024), BF16), vmem((1024, 512), F32), vmem((512, 1024), F32),
+        vmem((8, 1024), F32),
     )
     scratch = [
         vmem((8, 1024), BF16), vmem((8, 1024), BF16), vmem((1024, 512), BF16), vmem((512, 1024), BF16),
         vmem((1, 1024), F32), vmem((1, 512), F32), vmem((1, 512), F32), vmem((1, 1024), F32),
-        vmem((8, 1024), BF16), vmem((1024, 512), F32), vmem((512, 1024), F32), vmem((8, 1024), F32),
         vmem((NZ, NY, 16, FIRST), BF16), vmem((NZ, NY, 16, 1024 - FIRST), BF16),
         vmem((512, 1024), BF16), vmem((512, 1024), BF16),
         vmem((512, 512), BF16), vmem((512, 512), BF16),
@@ -576,7 +564,7 @@
         vmem((NY, 16, 128), F32), vmem((NZ, 16, 128), BF16),
         vmem((NY, 16, 128), F32), vmem((NZ, 16, 128), BF16),
         vmem((8, 8, 128), F32), vmem((8, 8, 128), F32),
-        dma((8,)), dma((4,)),
+        dma((8,)),
         dma((NY,)), dma((NY,)), dma((2, 9, NY)), dma((2, 9, NY)),
         dma((2, 9, NY)), dma((2, 9, NY)), dma((2, 9)), dma((2, 9)), dma((8,)), dma((8,)),
         dma((8, NX)), dma((8, NX)), dma((8, 8)), dma((8, 8)),
@@ -588,11 +576,11 @@
     return pl.pallas_call(
         kernel,
         out_shape=outs,
-        in_specs=[ANY_SPEC] * 8,
-        out_specs=[ANY_SPEC] * 4,
+        in_specs=[pl.BlockSpec(memory_space=pltpu.HBM)] * 8,
+        out_specs=[VMEM_SPEC] * 4,
         scratch_shapes=scratch,
         compiler_params=pltpu.CompilerParams(
-            collective_id=1, has_side_effects=True, vmem_limit_bytes=56 * 2**20
+            collective_id=1, has_side_effects=True, vmem_limit_bytes=52 * 2**20
         ),
         cost_estimate=pl.CostEstimate(
             flops=2700000000, bytes_accessed=8 * 2**20, transcendentals=100000
@@ -617,10 +605,14 @@
 
     inv_in = vec_ref[3:4, 0:512]
     inv_out = vec_ref[3:4, 512:1024]
-    uin_ref[...] = (gin_ref[...] * inv_in).astype(BF16)
+    many, few = 1024 // STEPS, 512 // STEPS
+    step_id = pl.program_id(0)
+    rows = pl.ds(pl.multiple_of(step_id * many, many), many)
+    uin_ref[...] = (gin_ref[rows, :] * inv_in).astype(BF16)
+    rows = pl.ds(pl.multiple_of(step_id * few, few), few)
     for k in range(2):
         lanes = slice(k * 512, (k + 1) * 512)
-        uout_ref[:, lanes] = (gout_ref[:, lanes] * inv_out).astype(BF16)
+        uout_ref[:, lanes] = (gout_ref[rows, lanes] * inv_out).astype(BF16)
 
 
 def scale(*args):
@@ -631,7 +623,7 @@
         scale_kernel,
         grid=(STEPS,),
         in_specs=[
-            whole(8, 1024), big(1024 // STEPS, 512), big(512 // STEPS, 1024), whole(8, 1024),
+            VMEM_SPEC, VMEM_SPEC, VMEM_SPEC, VMEM_SPEC,
         ],
         out_specs=[
             whole(8, 1024), big(1024 // STEPS, 512), big(512 // STEPS, 1024),
@@ -641,7 +633,7 @@
             shape((8, 1024), BF16), shape((1024, 512), BF16), shape((512, 1024), BF16),
             shape((8, 128), F32), shape((4, 128), F32), shape((4, 128), F32), shape((8, 128), F32),
         ),
-        compiler_params=pltpu.CompilerParams(vmem_limit_bytes=56 * 2**20),
+        compiler_params=pltpu.CompilerParams(vmem_limit_bytes=48 * 2**20),
     )(*args)
 
 

time: 83.9 us -> 81.5 us (0.971)
  Pallas kernels: 83.1 us -> 80.6 us
    pallas_call x2, Pallas kernels: 83.1 us -> 80.6 us  [the longest x1 79.1 us: step(): pl.pallas_call(kernel, out_shape=outs, in_specs=[pl.BlockSpec(memory_spac...]
where the time goes in v6:
time: 81.5 us; the launch traced here: 81.3 us
  Pallas kernels  80.6 us (99%)
    pallas_call x1, Pallas kernels, step(): pl.pallas_call(kernel, out_shape=outs, in_specs=[pl.BlockSpec(memory_spac...  79.1 us

profile of v6, /device:TPU:1, one launch (start us, length us, event | category | flops | bytes accessed | tf_op | source)
XLA Modules:
  0.0 81.3 jit_solution(5102754685072348285)
XLA Ops:
  0.6 79.1 %shard_map.135 = (bf16[8,1024]{1,0:T(8,128)(2,1)S(1)}, f32[1024,512]{1,0:T(8,128)S(1)}, f32[512,1024]{1,0:T(8,128)S(1)}, f32[8,1024]{1,0:T(8,128)S(1)}) custom-call(bf16[8,1024]{1,0:T(8,128)(2,1)} %x_hbm.1, bf16[8,1024]{1,0:T(8,128)(2,1)} %dy_hbm.1, bf16[1024,512]{1,0:T(8,128)(2,1)} %win_hbm.1, bf16[512,1024]{1,0:T(8,128)(2,1)} %wout_hbm.1, ...), custom_call_target="tpu_custom_call" | custom-call | flops 2700000000 | bytes 8388608 | tf_op jit(solution)/shard_map/pallas_call | solution.py:576
  79.8 1.5 %shard_map.136 = (bf16[8,1024]{1,0:T(8,128)(2,1)}, bf16[1024,512]{1,0:T(8,128)(2,1)}, bf16[512,1024]{1,0:T(8,128)(2,1)}, f32[8,128]{1,0:T(8,128)}, f32[4,128]{1,...) custom-call(bf16[8,1024]{1,0:T(8,128)(2,1)S(1)} %get-tuple-element.18.ig_ref, f32[1024,512]{1,0:T(8,128)S(1)} %get-tuple-element.19.gin_ref, ...), custom_call_target="tpu_custom_call" | custom-call | tf_op jit(solution)/shard_map/pallas_call | solution.py:622
